TPU v7x, 256 devices: a whole 4x4x8 slice. The times are simulated.
256 devices in a mesh: dp: 4 (over y), outer: 8 (over z_hi, x), inner: 8 (over z_lo, core).
Axes of the slice: x: 4, y: 4, z: 8 (z_hi: 2, z_lo: 4; z = z_hi * 4 + z_lo), core: 2. Of those that a mesh axis runs over, the one named last changes fastest.
Arguments:
- query_states: bfloat16 [65536, 1024], P(('dp', 'outer', 'inner')), parts along dimension 0, may hold values from -6 to 6
- key_states: bfloat16 [65536, 256], P(('dp', 'outer', 'inner')), parts along dimension 0, may hold values from -6 to 6
- value_states: bfloat16 [65536, 256], P(('dp', 'outer', 'inner')), parts along dimension 0, may hold values from -6 to 6
- out_grad: bfloat16 [65536, 1024], P(('dp', 'outer', 'inner')), parts along dimension 0, may hold values from -6 to 6
- cu_seqlens: int32 [260], P('dp'), parts along dimension 0, may hold values from 0 to 16384, as said below
Outputs:
- query_grad: bfloat16 [65536, 1024], P(('dp', 'outer', 'inner')), parts along dimension 0
- key_grad: bfloat16 [65536, 256], P(('dp', 'outer', 'inner')), parts along dimension 0
- value_grad: bfloat16 [65536, 256], P(('dp', 'outer', 'inner')), parts along dimension 0
There are 4 independent parts, one for each index of `dp`. A program takes and returns all parts, laid end to end along the dimension named above; each array names one. Nothing has to cross between parts.
Inputs may be any that keep to these rules, and one draw needn't show every extreme that they name: `cu_seqlens`: entries never fall, the first is 0 and the last is 16384; consecutive entries differ by at most 2048; trailing entries may repeat 16384.
All inputs are finite; a program needn't handle non-finite values.
Results may differ from a plain program's by a relative error of at most 0.024.
Values may be sent and summed in bfloat16 or wider, within the bound.
A program may use at most 128 MiB of HBM per device.

v0:
```python
import jax
import jax.numpy as jnp
from jax import lax
from jax.sharding import PartitionSpec as P

HEADS = 8
KV_HEADS = 2
HEAD_DIM = 128
HOPS = 8


def passed_along(value, axis, steps):
    count = lax.axis_size(axis)
    first, last = (max(0, -steps), min(count, count - steps))
    return lax.ppermute(value, axis, [(source, source + steps) for source in range(first, last)])


def doc_index(positions, cu_seqlens):
    return jnp.sum((cu_seqlens[1:][None, :] <= positions[:, None]).astype(jnp.int32), axis=1)


def block_scores(q_grouped, key_block, visible, score_scale):
    key_heads = key_block.reshape(key_block.shape[0], q_grouped.shape[1], q_grouped.shape[3])
    scores = (
        jnp.einsum("qgrd,kgd->grqk", q_grouped, key_heads, preferred_element_type=jnp.float32)
        * score_scale
    )
    return (jnp.where(visible, scores, jnp.float32(-1e30)), key_heads)


def per_device(query_states, key_states, value_states, out_grad, cu_seqlens):
    tok_rows = query_states.shape[0]
    group_size = HEADS // KV_HEADS
    score_scale = HEAD_DIM ** (-0.5)
    my_index = lax.axis_index(("outer", "inner"))
    local_pos = jnp.arange(tok_rows, dtype=jnp.int32)
    q_grouped = query_states.reshape(tok_rows, KV_HEADS, group_size, HEAD_DIM)
    g_grouped = out_grad.reshape(tok_rows, KV_HEADS, group_size, HEAD_DIM)
    query_pos = my_index * tok_rows + local_pos
    query_doc = doc_index(query_pos, cu_seqlens)
    blocks = [(key_states, value_states)]
    for hop_index in range(1, HOPS + 1):
        blocks.append(passed_along((key_states, value_states), ("outer", "inner"), hop_index))
    score_list = []
    heads_list = []
    run_max = None
    run_sum = None
    for hop_index in range(HOPS + 1):
        src_index = my_index - hop_index
        key_pos = src_index * tok_rows + local_pos
        key_doc = doc_index(key_pos, cu_seqlens)
        visible = (
            (key_pos[None, :] <= query_pos[:, None])
            & (key_doc[None, :] == query_doc[:, None])
            & (src_index >= 0)
        )
        scores, key_heads = block_scores(q_grouped, blocks[hop_index][0], visible, score_scale)
        score_list.append(scores)
        heads_list.append(key_heads)
        block_max = jnp.max(scores, axis=-1)
        if hop_index == 0:
            run_max = block_max
            run_sum = jnp.sum(jnp.exp(scores - run_max[..., None]), axis=-1)
        else:
            new_max = jnp.maximum(run_max, block_max)
            run_sum = run_sum * jnp.exp(run_max - new_max) + jnp.sum(
                jnp.exp(scores - new_max[..., None]), axis=-1
            )
            run_max = new_max
    log_norm = run_max + jnp.log(run_sum)
    prob_list = []
    attn_out = jnp.zeros((tok_rows, KV_HEADS, group_size, HEAD_DIM), jnp.float32)
    for hop_index in range(HOPS + 1):
        probs = jnp.exp(score_list[hop_index] - log_norm[..., None])
        prob_list.append(probs)
        probs16 = probs.astype(jnp.bfloat16)
        value_heads = blocks[hop_index][1].reshape(tok_rows, KV_HEADS, HEAD_DIM)
        attn_out = attn_out + jnp.einsum(
            "grqk,kgd->qgrd", probs16, value_heads, preferred_element_type=jnp.float32
        )
    row_delta = jnp.einsum("qgrd,qgrd->grq", g_grouped.astype(jnp.float32), attn_out)
    query_acc = jnp.zeros((tok_rows, KV_HEADS, group_size, HEAD_DIM), jnp.float32)
    grad_parts = []
    for hop_index in range(HOPS + 1):
        probs = prob_list[hop_index]
        probs16 = probs.astype(jnp.bfloat16)
        key_heads = heads_list[hop_index]
        value_heads = blocks[hop_index][1].reshape(tok_rows, KV_HEADS, HEAD_DIM)
        prob_grad = jnp.einsum(
            "qgrd,kgd->grqk", g_grouped, value_heads, preferred_element_type=jnp.float32
        )
        score_grad = (probs * (prob_grad - row_delta[..., None])).astype(jnp.bfloat16)
        query_acc = query_acc + jnp.einsum(
            "grqk,kgd->qgrd", score_grad, key_heads, preferred_element_type=jnp.float32
        )
        key_part = (
            jnp.einsum("grqk,qgrd->kgd", score_grad, q_grouped, preferred_element_type=jnp.float32)
            * score_scale
        )
        value_part = jnp.einsum(
            "grqk,qgrd->kgd", probs16, g_grouped, preferred_element_type=jnp.float32
        )
        grad_parts.append(
            (
                key_part.reshape(tok_rows, KV_HEADS * HEAD_DIM),
                value_part.reshape(tok_rows, KV_HEADS * HEAD_DIM),
            )
        )
    query_grad = (query_acc * score_scale).reshape(tok_rows, HEADS * HEAD_DIM).astype(jnp.bfloat16)
    acc_k, acc_v = grad_parts[0]
    for hop_index in range(1, HOPS + 1):
        back_k, back_v = (
            passed_along(
                grad_parts[hop_index][0].astype(jnp.bfloat16), ("outer", "inner"), -hop_index
            ).astype(jnp.float32),
            passed_along(
                grad_parts[hop_index][1].astype(jnp.bfloat16), ("outer", "inner"), -hop_index
            ).astype(jnp.float32),
        )
        acc_k = acc_k + back_k
        acc_v = acc_v + back_v
    return (query_grad, acc_k.astype(jnp.bfloat16), acc_v.astype(jnp.bfloat16))


def solution(mesh):
    return jax.shard_map(
        per_device,
        mesh=mesh,
        in_specs=(
            P(("dp", "outer", "inner"), None),
            P(("dp", "outer", "inner"), None),
            P(("dp", "outer", "inner"), None),
            P(("dp", "outer", "inner"), None),
            P("dp"),
        ),
        out_specs=(
            P(("dp", "outer", "inner"), None),
            P(("dp", "outer", "inner"), None),
            P(("dp", "outer", "inner"), None),
        ),
        check_vma=False,
    )
```

profile of v0, /device:TPU:62, one launch (start us, length us, event | category | flops | bytes accessed | tf_op | source)
XLA Modules:
  0.0 316.0 jit_solution(11641856757044123153)
XLA Ops:
  2.4 8.1 %collective-permute-start.15 = (bf16[256,256]{0,1:T(8,128)(2,1)}, bf16[256,256]{0,1:T(8,128)(2,1)}, u32[]{:S(2)}, u32[]{:S(2)}) collective-permute-start(bf16[256,256]{0,1:T(8,128)(2,1)} %copy.248), channel_id=1, source_target_pairs={{0,8},{1,9},{2,10},{3,11},{4,12},{5,13},{6,14},{7,15},{8,16},{9,17... | collective-permute-start | bytes 393224 | tf_op jit(solution)/shard_map/ppermute | solution.py:15
  12.6 3.8 %collective-permute-start.13 = (bf16[256,256]{0,1:T(8,128)(2,1)}, bf16[256,256]{0,1:T(8,128)(2,1)}, u32[]{:S(2)}, u32[]{:S(2)}) collective-permute-start(bf16[256,256]{0,1:T(8,128)(2,1)} %copy.248), channel_id=1, source_target_pairs={{0,6},{1,7},{2,8},{3,9},{4,10},{5,11},{6,12},{7,13},{8,14},{9,15},... | collective-permute-start | bytes 393224 | tf_op jit(solution)/shard_map/ppermute | solution.py:15
  16.4 3.2 %collective-permute-start.12 = (bf16[256,256]{0,1:T(8,128)(2,1)}, bf16[256,256]{0,1:T(8,128)(2,1)}, u32[]{:S(2)}, u32[]{:S(2)}) collective-permute-start(bf16[256,256]{0,1:T(8,128)(2,1)} %copy.248), channel_id=1, source_target_pairs={{0,5},{1,6},{2,7},{3,8},{4,9},{5,10},{6,11},{7,12},{8,13},{9,14},{... | collective-permute-start | bytes 393224 | tf_op jit(solution)/shard_map/ppermute | solution.py:15
  21.3 4.0 %collective-permute-start.7 = (bf16[256,256]{0,1:T(8,128)(2,1)}, bf16[256,256]{0,1:T(8,128)(2,1)S(1)}, u32[]{:S(2)}, u32[]{:S(2)}) collective-permute-start(bf16[256,256]{0,1:T(8,128)(2,1)} %copy.220), channel_id=1, source_target_pairs={{0,8},{1,9},{2,10},{3,11},{4,12},{5,13},{6,14},{7,15},{8,16},{9,17... | collective-permute-start | bytes 393224 | tf_op jit(solution)/shard_map/ppermute | solution.py:15
  32.9 5.8 %collective-permute-start.6 = (bf16[256,256]{0,1:T(8,128)(2,1)}, bf16[256,256]{0,1:T(8,128)(2,1)S(1)}, u32[]{:S(2)}, u32[]{:S(2)}) collective-permute-start(bf16[256,256]{0,1:T(8,128)(2,1)} %copy.220), channel_id=1, source_target_pairs={{0,7},{1,8},{2,9},{3,10},{4,11},{5,12},{6,13},{7,14},{8,15},{9,16}... | collective-permute-start | bytes 393224 | tf_op jit(solution)/shard_map/ppermute | solution.py:15
  39.2 3.7 %collective-permute-done.6 = bf16[256,256]{0,1:T(8,128)(2,1)S(1)} collective-permute-done((bf16[256,256]{0,1:T(8,128)(2,1)}, bf16[256,256]{0,1:T(8,128)(2,1)S(1)}, u32[]{:S(2)}, u32[]{:S(2)}) %collective-permute-start.6) | collective-permute-done | bytes 131104 | tf_op jit(solution)/shard_map/ppermute | solution.py:15
  42.9 9.0 %collective-permute-start.5 = (bf16[256,256]{0,1:T(8,128)(2,1)}, bf16[256,256]{0,1:T(8,128)(2,1)S(1)}, u32[]{:S(2)}, u32[]{:S(2)}) collective-permute-start(bf16[256,256]{0,1:T(8,128)(2,1)} %copy.220), channel_id=1, source_target_pairs={{0,6},{1,7},{2,8},{3,9},{4,10},{5,11},{6,12},{7,13},{8,14},{9,15},... | collective-permute-start | bytes 393224 | tf_op jit(solution)/shard_map/ppermute | solution.py:15
  52.5 2.9 collective-permute-done.5
  55.4 21.3 %collective-permute-start.4 = (bf16[256,256]{0,1:T(8,128)(2,1)}, bf16[256,256]{0,1:T(8,128)(2,1)S(1)}, u32[]{:S(2)}, u32[]{:S(2)}) collective-permute-start(bf16[256,256]{0,1:T(8,128)(2,1)} %copy.220), channel_id=1, source_target_pairs={{0,5},{1,6},{2,7},{3,8},{4,9},{5,10},{6,11},{7,12},{8,13},{9,14},{... | collective-permute-start | bytes 393224 | tf_op jit(solution)/shard_map/ppermute | solution.py:15
  77.2 2.3 collective-permute-done.4
  79.5 10.0 %collective-permute-start.3 = (bf16[256,256]{0,1:T(8,128)(2,1)}, bf16[256,256]{0,1:T(8,128)(2,1)S(1)}, u32[]{:S(2)}, u32[]{:S(2)}) collective-permute-start(bf16[256,256]{0,1:T(8,128)(2,1)} %copy.220), channel_id=1, source_target_pairs={{0,4},{1,5},{2,6},{3,7},{4,8},{5,9},{6,10},{7,11},{8,12},{9,13},{1... | collective-permute-start | bytes 393224 | tf_op jit(solution)/shard_map/ppermute | solution.py:15
  94.8 7.2 %collective-permute-done.2 = bf16[256,256]{0,1:T(8,128)(2,1)S(1)} collective-permute-done((bf16[256,256]{0,1:T(8,128)(2,1)}, bf16[256,256]{0,1:T(8,128)(2,1)S(1)}, u32[]{:S(2)}, u32[]{:S(2)}) %collective-permute-start.2) | collective-permute-done | bytes 131104 | tf_op jit(solution)/shard_map/ppermute | solution.py:15
  102.0 2.6 collective-permute-start.1
  105.1 4.0 %collective-permute-done.1 = bf16[256,256]{0,1:T(8,128)(2,1)S(1)} collective-permute-done((bf16[256,256]{0,1:T(8,128)(2,1)}, bf16[256,256]{0,1:T(8,128)(2,1)S(1)}, u32[]{:S(2)}, u32[]{:S(2)}) %collective-permute-start.1) | collective-permute-done | bytes 131104 | tf_op jit(solution)/shard_map/ppermute | solution.py:15
  109.1 5.4 %collective-permute-start = (bf16[256,256]{0,1:T(8,128)(2,1)}, bf16[256,256]{0,1:T(8,128)(2,1)S(1)}, u32[]{:S(2)}, u32[]{:S(2)}) collective-permute-start(bf16[256,256]{0,1:T(8,128)(2,1)} %copy.220), channel_id=1, source_target_pairs={{0,1},{1,2},{2,3},{3,4},{4,5},{5,6},{6,7},{7,8},{8,9},{9,10},{10,1... | collective-permute-start | bytes 393224 | tf_op jit(solution)/shard_map/ppermute | solution.py:15
  116.5 9.8 %collective-permute-start.10 = (bf16[256,256]{0,1:T(8,128)(2,1)}, bf16[256,256]{0,1:T(8,128)(2,1)S(1)}, u32[]{:S(2)}, u32[]{:S(2)}) collective-permute-start(bf16[256,256]{0,1:T(8,128)(2,1)} %copy.248), channel_id=1, source_target_pairs={{0,3},{1,4},{2,5},{3,6},{4,7},{5,8},{6,9},{7,10},{8,11},{9,12},{10... | collective-permute-start | bytes 393224 | tf_op jit(solution)/shard_map/ppermute | solution.py:15
  131.7 6.2 %collective-permute-start.11 = (bf16[256,256]{0,1:T(8,128)(2,1)}, bf16[256,256]{0,1:T(8,128)(2,1)S(1)}, u32[]{:S(2)}, u32[]{:S(2)}) collective-permute-start(bf16[256,256]{0,1:T(8,128)(2,1)} %copy.248), channel_id=1, source_target_pairs={{0,4},{1,5},{2,6},{3,7},{4,8},{5,9},{6,10},{7,11},{8,12},{9,13},{1... | collective-permute-start | bytes 393224 | tf_op jit(solution)/shard_map/ppermute | solution.py:15
  141.8 11.0 %collective-permute-start.9 = (bf16[256,256]{0,1:T(8,128)(2,1)}, bf16[256,256]{0,1:T(8,128)(2,1)S(1)}, u32[]{:S(2)}, u32[]{:S(2)}) collective-permute-start(bf16[256,256]{0,1:T(8,128)(2,1)} %copy.248), channel_id=1, source_target_pairs={{0,2},{1,3},{2,4},{3,5},{4,6},{5,7},{6,8},{7,9},{8,10},{9,11},{10,... | collective-permute-start | bytes 393224 | tf_op jit(solution)/shard_map/ppermute | solution.py:15
  173.6 3.4 %fusion.15 = bf16[2,4,256,256]{2,3,1,0:T(8,128)(2,1)} fusion(f32[2,4,256,256]{2,3,1,0:T(8,128)} %copy-done.12, bf16[256,2,128,1]{0,2,3,1:T(8,128)(2,1)} %bitcast.569, bf16[256,2,4,128]{0,3,2,1:T(8,128)(2,1)S(1)} %copy.326, f32[2,4,256]{2,1,0:T(4,128)S(1)} %copy.387, f32[2,4,256]{2,1,0:T(4,128)S(1)} %bitcast.515), kind=kOutput, calls=%fused_computation.23 | convolution fusion | flops 136314880 | bytes 3817472 | tf_op jit(solution)/shard_map/qgrd,kgd->grqk/dot_general | solution.py:89
  213.7 3.3 %collective-permute-start.27 = (bf16[256,256]{1,0:T(8,128)(2,1)}, bf16[256,256]{1,0:T(8,128)(2,1)}, u32[]{:S(2)}, u32[]{:S(2)}) collective-permute-start(bf16[256,256]{1,0:T(8,128)(2,1)} %copy.339), channel_id=1, source_target_pairs={{4,0},{5,1},{6,2},{7,3},{8,4},{9,5},{10,6},{11,7},{12,8},{13,9},{1... | collective-permute-start | bytes 393224 | tf_op jit(solution)/shard_map/ppermute | solution.py:15
  238.3 8.1 %collective-permute-done.30 = bf16[256,256]{1,0:T(8,128)(2,1)} collective-permute-done((bf16[256,256]{1,0:T(8,128)(2,1)}, bf16[256,256]{1,0:T(8,128)(2,1)}, u32[]{:S(2)}, u32[]{:S(2)}) %collective-permute-start.30) | collective-permute-done | bytes 131104 | tf_op jit(solution)/shard_map/ppermute | solution.py:15
  258.5 4.4 %collective-permute-done.25 = bf16[256,256]{1,0:T(8,128)(2,1)} collective-permute-done((bf16[256,256]{1,0:T(8,128)(2,1)}, bf16[256,256]{1,0:T(8,128)(2,1)}, u32[]{:S(2)}, u32[]{:S(2)}) %collective-permute-start.25) | collective-permute-done | bytes 131104 | tf_op jit(solution)/shard_map/ppermute | solution.py:15
  279.9 18.9 %collective-permute-done.21 = bf16[256,256]{1,0:T(8,128)(2,1)S(1)} collective-permute-done((bf16[256,256]{1,0:T(8,128)(2,1)S(1)}, bf16[256,256]{1,0:T(8,128)(2,1)S(1)}, u32[]{:S(2)}, u32[]{:S(2)}) %collective-permute-start.21) | collective-permute-done | bytes 131104 | tf_op jit(solution)/shard_map/ppermute | solution.py:15
  301.0 13.2 %collective-permute-done.23 = bf16[256,256]{1,0:T(8,128)(2,1)S(1)} collective-permute-done((bf16[256,256]{1,0:T(8,128)(2,1)S(1)}, bf16[256,256]{1,0:T(8,128)(2,1)S(1)}, u32[]{:S(2)}, u32[]{:S(2)}) %collective-permute-start.23) | collective-permute-done | bytes 131104 | tf_op jit(solution)/shard_map/ppermute | solution.py:15
  (251 shorter events, 142.7 us)
Async XLA Ops:
  2.4 162.2 %collective-permute-start.15 = (bf16[256,256]{0,1:T(8,128)(2,1)}, bf16[256,256]{0,1:T(8,128)(2,1)}, u32[]{:S(2)}, u32[]{:S(2)}) collective-permute-start(bf16[256,256]{0,1:T(8,128)(2,1)} %copy.248), channel_id=1, source_target_pairs={{0,8},{1,9},{2,10},{3,11},{4,12},{5,13},{6,14},{7,15},{8,16},{9,17... | collective-permute-start | bytes 393224 | tf_op jit(solution)/shard_map/ppermute | solution.py:15
  10.5 151.5 %collective-permute-start.14 = (bf16[256,256]{0,1:T(8,128)(2,1)}, bf16[256,256]{0,1:T(8,128)(2,1)}, u32[]{:S(2)}, u32[]{:S(2)}) collective-permute-start(bf16[256,256]{0,1:T(8,128)(2,1)} %copy.248), channel_id=1, source_target_pairs={{0,7},{1,8},{2,9},{3,10},{4,11},{5,12},{6,13},{7,14},{8,15},{9,16}... | collective-permute-start | bytes 393224 | tf_op jit(solution)/shard_map/ppermute | solution.py:15
  12.6 146.7 %collective-permute-start.13 = (bf16[256,256]{0,1:T(8,128)(2,1)}, bf16[256,256]{0,1:T(8,128)(2,1)}, u32[]{:S(2)}, u32[]{:S(2)}) collective-permute-start(bf16[256,256]{0,1:T(8,128)(2,1)} %copy.248), channel_id=1, source_target_pairs={{0,6},{1,7},{2,8},{3,9},{4,10},{5,11},{6,12},{7,13},{8,14},{9,15},... | collective-permute-start | bytes 393224 | tf_op jit(solution)/shard_map/ppermute | solution.py:15
  16.4 138.1 %collective-permute-start.12 = (bf16[256,256]{0,1:T(8,128)(2,1)}, bf16[256,256]{0,1:T(8,128)(2,1)}, u32[]{:S(2)}, u32[]{:S(2)}) collective-permute-start(bf16[256,256]{0,1:T(8,128)(2,1)} %copy.248), channel_id=1, source_target_pairs={{0,5},{1,6},{2,7},{3,8},{4,9},{5,10},{6,11},{7,12},{8,13},{9,14},{... | collective-permute-start | bytes 393224 | tf_op jit(solution)/shard_map/ppermute | solution.py:15
  55.4 24.1 %collective-permute-start.4 = (bf16[256,256]{0,1:T(8,128)(2,1)}, bf16[256,256]{0,1:T(8,128)(2,1)S(1)}, u32[]{:S(2)}, u32[]{:S(2)}) collective-permute-start(bf16[256,256]{0,1:T(8,128)(2,1)} %copy.220), channel_id=1, source_target_pairs={{0,5},{1,6},{2,7},{3,8},{4,9},{5,10},{6,11},{7,12},{8,13},{9,14},{... | collective-permute-start | bytes 393224 | tf_op jit(solution)/shard_map/ppermute | solution.py:15
  116.5 15.2 %collective-permute-start.10 = (bf16[256,256]{0,1:T(8,128)(2,1)}, bf16[256,256]{0,1:T(8,128)(2,1)S(1)}, u32[]{:S(2)}, u32[]{:S(2)}) collective-permute-start(bf16[256,256]{0,1:T(8,128)(2,1)} %copy.248), channel_id=1, source_target_pairs={{0,3},{1,4},{2,5},{3,6},{4,7},{5,8},{6,9},{7,10},{8,11},{9,12},{10... | collective-permute-start | bytes 393224 | tf_op jit(solution)/shard_map/ppermute | solution.py:15
  141.8 27.9 %collective-permute-start.9 = (bf16[256,256]{0,1:T(8,128)(2,1)}, bf16[256,256]{0,1:T(8,128)(2,1)S(1)}, u32[]{:S(2)}, u32[]{:S(2)}) collective-permute-start(bf16[256,256]{0,1:T(8,128)(2,1)} %copy.248), channel_id=1, source_target_pairs={{0,2},{1,3},{2,4},{3,5},{4,6},{5,7},{6,8},{7,9},{8,10},{9,11},{10,... | collective-permute-start | bytes 393224 | tf_op jit(solution)/shard_map/ppermute | solution.py:15
  154.5 13.3 %collective-permute-start.8 = (bf16[256,256]{0,1:T(8,128)(2,1)}, bf16[256,256]{0,1:T(8,128)(2,1)S(1)}, u32[]{:S(2)}, u32[]{:S(2)}) collective-permute-start(bf16[256,256]{0,1:T(8,128)(2,1)} %copy.248), channel_id=1, source_target_pairs={{0,1},{1,2},{2,3},{3,4},{4,5},{5,6},{6,7},{7,8},{8,9},{9,10},{10,1... | collective-permute-start | bytes 393224 | tf_op jit(solution)/shard_map/ppermute | solution.py:15
  207.9 20.2 %collective-permute-start.31 = (bf16[256,256]{1,0:T(8,128)(2,1)}, bf16[256,256]{1,0:T(8,128)(2,1)}, u32[]{:S(2)}, u32[]{:S(2)}) collective-permute-start(bf16[256,256]{1,0:T(8,128)(2,1)} %copy.351), channel_id=1, source_target_pairs={{8,0},{9,1},{10,2},{11,3},{12,4},{13,5},{14,6},{15,7},{16,8},{17,9... | collective-permute-start | bytes 393224 | tf_op jit(solution)/shard_map/ppermute | solution.py:15
  209.9 38.5 %collective-permute-start.29 = (bf16[256,256]{1,0:T(8,128)(2,1)}, bf16[256,256]{1,0:T(8,128)(2,1)}, u32[]{:S(2)}, u32[]{:S(2)}) collective-permute-start(bf16[256,256]{1,0:T(8,128)(2,1)} %copy.345), channel_id=1, source_target_pairs={{6,0},{7,1},{8,2},{9,3},{10,4},{11,5},{12,6},{13,7},{14,8},{15,9},... | collective-permute-start | bytes 393224 | tf_op jit(solution)/shard_map/ppermute | solution.py:15
  211.8 38.5 %collective-permute-start.28 = (bf16[256,256]{1,0:T(8,128)(2,1)}, bf16[256,256]{1,0:T(8,128)(2,1)}, u32[]{:S(2)}, u32[]{:S(2)}) collective-permute-start(bf16[256,256]{1,0:T(8,128)(2,1)} %copy.342), channel_id=1, source_target_pairs={{5,0},{6,1},{7,2},{8,3},{9,4},{10,5},{11,6},{12,7},{13,8},{14,9},{... | collective-permute-start | bytes 393224 | tf_op jit(solution)/shard_map/ppermute | solution.py:15
  213.7 38.5 %collective-permute-start.27 = (bf16[256,256]{1,0:T(8,128)(2,1)}, bf16[256,256]{1,0:T(8,128)(2,1)}, u32[]{:S(2)}, u32[]{:S(2)}) collective-permute-start(bf16[256,256]{1,0:T(8,128)(2,1)} %copy.339), channel_id=1, source_target_pairs={{4,0},{5,1},{6,2},{7,3},{8,4},{9,5},{10,6},{11,7},{12,8},{13,9},{1... | collective-permute-start | bytes 393224 | tf_op jit(solution)/shard_map/ppermute | solution.py:15
  226.3 20.2 %collective-permute-start.30 = (bf16[256,256]{1,0:T(8,128)(2,1)}, bf16[256,256]{1,0:T(8,128)(2,1)}, u32[]{:S(2)}, u32[]{:S(2)}) collective-permute-start(bf16[256,256]{1,0:T(8,128)(2,1)} %copy.348), channel_id=1, source_target_pairs={{7,0},{8,1},{9,2},{10,3},{11,4},{12,5},{13,6},{14,7},{15,8},{16,9}... | collective-permute-start | bytes 393224 | tf_op jit(solution)/shard_map/ppermute | solution.py:15
  228.2 26.0 %collective-permute-start.26 = (bf16[256,256]{1,0:T(8,128)(2,1)}, bf16[256,256]{1,0:T(8,128)(2,1)}, u32[]{:S(2)}, u32[]{:S(2)}) collective-permute-start(bf16[256,256]{1,0:T(8,128)(2,1)} %copy.336), channel_id=1, source_target_pairs={{3,0},{4,1},{5,2},{6,3},{7,4},{8,5},{9,6},{10,7},{11,8},{12,9},{13... | collective-permute-start | bytes 393224 | tf_op jit(solution)/shard_map/ppermute | solution.py:15
  246.4 16.5 %collective-permute-start.25 = (bf16[256,256]{1,0:T(8,128)(2,1)}, bf16[256,256]{1,0:T(8,128)(2,1)}, u32[]{:S(2)}, u32[]{:S(2)}) collective-permute-start(bf16[256,256]{1,0:T(8,128)(2,1)} %copy.333), channel_id=1, source_target_pairs={{2,0},{3,1},{4,2},{5,3},{6,4},{7,5},{8,6},{9,7},{10,8},{11,9},{12,... | collective-permute-start | bytes 393224 | tf_op jit(solution)/shard_map/ppermute | solution.py:15
  248.4 16.5 %collective-permute-start.24 = (bf16[256,256]{1,0:T(8,128)(2,1)}, bf16[256,256]{1,0:T(8,128)(2,1)}, u32[]{:S(2)}, u32[]{:S(2)}) collective-permute-start(bf16[256,256]{1,0:T(8,128)(2,1)} %copy.329), channel_id=1, source_target_pairs={{1,0},{2,1},{3,2},{4,3},{5,4},{6,5},{7,6},{8,7},{9,8},{10,9},{11,1... | collective-permute-start | bytes 393224 | tf_op jit(solution)/shard_map/ppermute | solution.py:15
  250.3 16.5 %collective-permute-start.16 = (bf16[256,256]{1,0:T(8,128)(2,1)}, bf16[256,256]{1,0:T(8,128)(2,1)}, u32[]{:S(2)}, u32[]{:S(2)}) collective-permute-start(bf16[256,256]{1,0:T(8,128)(2,1)} %copy.302), channel_id=1, source_target_pairs={{1,0},{2,1},{3,2},{4,3},{5,4},{6,5},{7,6},{8,7},{9,8},{10,9},{11,1... | collective-permute-start | bytes 393224 | tf_op jit(solution)/shard_map/ppermute | solution.py:15
  252.3 17.7 %collective-permute-start.17 = (bf16[256,256]{1,0:T(8,128)(2,1)S(1)}, bf16[256,256]{1,0:T(8,128)(2,1)}, u32[]{:S(2)}, u32[]{:S(2)}) collective-permute-start(bf16[256,256]{1,0:T(8,128)(2,1)S(1)} %copy.306), channel_id=1, source_target_pairs={{2,0},{3,1},{4,2},{5,3},{6,4},{7,5},{8,6},{9,7},{10,8},{11,9},{12,... | collective-permute-start | bytes 393224 | tf_op jit(solution)/shard_map/ppermute | solution.py:15
  254.2 19.0 %collective-permute-start.18 = (bf16[256,256]{1,0:T(8,128)(2,1)S(1)}, bf16[256,256]{1,0:T(8,128)(2,1)}, u32[]{:S(2)}, u32[]{:S(2)}) collective-permute-start(bf16[256,256]{1,0:T(8,128)(2,1)S(1)} %copy.309), channel_id=1, source_target_pairs={{3,0},{4,1},{5,2},{6,3},{7,4},{8,5},{9,6},{10,7},{11,8},{12,9},{13... | collective-permute-start | bytes 393224 | tf_op jit(solution)/shard_map/ppermute | solution.py:15
  262.9 14.8 %collective-permute-start.19 = (bf16[256,256]{1,0:T(8,128)(2,1)S(1)}, bf16[256,256]{1,0:T(8,128)(2,1)S(1)}, u32[]{:S(2)}, u32[]{:S(2)}) collective-permute-start(bf16[256,256]{1,0:T(8,128)(2,1)S(1)} %copy.312), channel_id=1, source_target_pairs={{4,0},{5,1},{6,2},{7,3},{8,4},{9,5},{10,6},{11,7},{12,8},{13,9},{1... | collective-permute-start | bytes 393224 | tf_op jit(solution)/shard_map/ppermute | solution.py:15
  264.8 15.1 %collective-permute-start.20 = (bf16[256,256]{1,0:T(8,128)(2,1)S(1)}, bf16[256,256]{1,0:T(8,128)(2,1)S(1)}, u32[]{:S(2)}, u32[]{:S(2)}) collective-permute-start(bf16[256,256]{1,0:T(8,128)(2,1)S(1)} %copy.315), channel_id=1, source_target_pairs={{5,0},{6,1},{7,2},{8,3},{9,4},{10,5},{11,6},{12,7},{13,8},{14,9},{... | collective-permute-start | bytes 393224 | tf_op jit(solution)/shard_map/ppermute | solution.py:15
  266.8 32.1 %collective-permute-start.21 = (bf16[256,256]{1,0:T(8,128)(2,1)S(1)}, bf16[256,256]{1,0:T(8,128)(2,1)S(1)}, u32[]{:S(2)}, u32[]{:S(2)}) collective-permute-start(bf16[256,256]{1,0:T(8,128)(2,1)S(1)} %copy.318), channel_id=1, source_target_pairs={{6,0},{7,1},{8,2},{9,3},{10,4},{11,5},{12,6},{13,7},{14,8},{15,9},... | collective-permute-start | bytes 393224 | tf_op jit(solution)/shard_map/ppermute | solution.py:15
  269.9 31.0 %collective-permute-start.22 = (bf16[256,256]{1,0:T(8,128)(2,1)S(1)}, bf16[256,256]{1,0:T(8,128)(2,1)S(1)}, u32[]{:S(2)}, u32[]{:S(2)}) collective-permute-start(bf16[256,256]{1,0:T(8,128)(2,1)S(1)} %copy.321), channel_id=1, source_target_pairs={{7,0},{8,1},{9,2},{10,3},{11,4},{12,5},{13,6},{14,7},{15,8},{16,9}... | collective-permute-start | bytes 393224 | tf_op jit(solution)/shard_map/ppermute | solution.py:15
  273.2 40.9 %collective-permute-start.23 = (bf16[256,256]{1,0:T(8,128)(2,1)S(1)}, bf16[256,256]{1,0:T(8,128)(2,1)S(1)}, u32[]{:S(2)}, u32[]{:S(2)}) collective-permute-start(bf16[256,256]{1,0:T(8,128)(2,1)S(1)} %copy.324), channel_id=1, source_target_pairs={{8,0},{9,1},{10,2},{11,3},{12,4},{13,5},{14,6},{15,7},{16,8},{17,9... | collective-permute-start | bytes 393224 | tf_op jit(solution)/shard_map/ppermute | solution.py:15
  (61 other events, 1102.3 us)
where the time goes:
time: 318 us; the launch traced here: 316 us
  starting transfers between devices  138 us (43%)
  waiting for transfers between devices  78 us (25%)
  matrix products  59 us (19%)
  local copies, waits for them, and re-layouts  29.5 us (9%)
  other arithmetic  9.56 us (3%)
    ppermute x32, starting transfers between devices, passed_along(): lax.ppermute(value, axis, [(source, source + steps) for source in range(f...  138 us
    ppermute x32, waiting for transfers between devices, passed_along(): lax.ppermute(value, axis, [(source, source + steps) for source in range(f...  78 us
    dot_general x9, matrix products, per_device(): jnp.einsum('qgrd,kgd->grqk', g_grouped, value_heads, preferred_element_ty...  13.9 us
    dot_general x9, matrix products, per_device(): jnp.einsum('grqk,kgd->qgrd', score_grad, key_heads, preferred_element_typ...  11.7 us
    convert_element_type x8, local copies, waits for them, and re-layouts, per_device(): grad_parts[hop_index][1].astype(jnp.bfloat16)  11.6 us
    dot_general x9, matrix products, per_device(): jnp.einsum('grqk,qgrd->kgd', probs16, g_grouped, preferred_element_type=j...  10.5 us
    dot_general x9, matrix products, per_device(): jnp.einsum('grqk,qgrd->kgd', score_grad, q_grouped, preferred_element_typ...  9.13 us
    dot_general x9, matrix products, per_device(): jnp.einsum('grqk,kgd->qgrd', probs16, value_heads, preferred_element_type...  8.89 us
  transfers between devices with their start and end apart: 32, of which 17 were waited for; matrix products, arithmetic and copies ran while one was open for 17% of the time, Pallas kernels for 0%

commit v1 on v0

v1 whole, which is shorter than its diff:
```python
import functools

import jax
import jax.numpy as jnp
from jax import lax
from jax.experimental import pallas as pl
from jax.experimental.pallas import tpu as pltpu
from jax.sharding import PartitionSpec as P

GROUP = 4
DIM = 128
TOK = 256
ROWS = 2 * TOK
SCALE = DIM**-0.5
TO_LOG2 = SCALE * 1.4426950408889634
HIDDEN = -1e30
MESH = pl.DeviceIdType.MESH
NT = (((1,), (1,)), ((), ()))
TN = (((0,), (0,)), ((), ()))

ORDERS = ((4, 3, 2, 1), (4, 1, 3, 2), (1, 4, 2, 3), (1, 2, 3, 4))
PACKED = sum(
    (distance - 1) * 4 ** (4 * row + 3 - place)
    for row, order in enumerate(ORDERS)
    for place, distance in enumerate(order)
)
LAG = 2


def dot(a, b, dims=(((1,), (0,)), ((), ()))):
    return lax.dot_general(a, b, dims, preferred_element_type=jnp.float32)


def kernel(
    cu_ref, q_in, k_in, v_in, g_in,
    dq_out, dk_out, dv_out,
    qbuf, gbuf, kbuf, vbuf, e_ref, d_ref, mu_ref, m_ref, l_ref, delta_ref, start_ref,
    part_ref, back_ref, give_ref, dqt_ref, dq_ref,
    local_sem, qg_send, qg_recv, kv_send, kv_recv, relay_send, back_send, back_recv, out_send, out_recv,
):
    outer, inner = lax.axis_index("outer"), lax.axis_index("inner")
    core = inner % 2
    z = inner // 2
    chip = outer * 4 + z
    fold = outer == 4
    up_there = (z < 3) | (outer == 3)
    down_there = (z > 0) | fold
    next_there = (outer != 3) & (outer != 7)
    last_there = (outer != 0) & (outer != 4)

    def device(which, side):
        return {"outer": which // 4, "inner": (which % 4) * 2 + side}

    sibling = device(chip, 1 - core)

    def from_below(slot):
        return (slot <= z) | fold

    def there(slot):
        return (slot <= z) | (outer != 0)

    def handed_on(slot):
        below = from_below(slot)
        return there(slot) & ((below & (slot < 4) & up_there) | (~below & (z > 0)))

    def arrival(place):
        row = jnp.where(fold, 3, jnp.minimum(z, 2))
        digits = PACKED // jnp.where(row == 0, 1, jnp.where(row == 1, 4**4, jnp.where(row == 2, 4**8, 4**12)))
        power = jnp.where(place == 0, 64, jnp.where(place == 1, 16, jnp.where(place == 2, 4, 1)))
        return (digits // power) % 4 + 1

    def half(side):
        return pl.ds(pl.multiple_of(side * TOK, TOK), TOK)

    def columns(first, count=DIM):
        return pl.ds(pl.multiple_of(first, DIM), count)

    local = []
    for r in range(GROUP):
        for n, (src, dst) in enumerate(((q_in, qbuf), (g_in, gbuf))):
            local.append(pltpu.make_async_copy(
                src.at[:, columns((core * GROUP + r) * DIM)], dst.at[r, half(core)], local_sem.at[n * GROUP + r]))
    for n, (src, dst) in enumerate(((k_in, kbuf), (v_in, vbuf))):
        local.append(pltpu.make_async_copy(
            src.at[:, columns(core * DIM)], dst.at[0, half(core)], local_sem.at[2 * GROUP + n]))
    for copy in local:
        copy.start()

    barrier = pltpu.get_barrier_semaphore()
    pl.semaphore_signal(barrier, 1, device_id=sibling, device_id_type=MESH)
    for is_there, other in ((up_there, chip + 1), (down_there, chip - 1), (next_there, chip + 4), (last_there, chip - 4)):
        @pl.when(is_there)
        def _(other=other):
            for side in range(2):
                pl.semaphore_signal(barrier, 1, device_id=device(other, side), device_id_type=MESH)
    pl.semaphore_wait(barrier, 1 + 2 * sum(
        jnp.where(is_there, 1, 0) for is_there in (up_there, down_there, next_there, last_there)))

    def remote(src, dst, send, recv, where):
        return pltpu.make_async_remote_copy(
            src_ref=src, dst_ref=dst, send_sem=send, recv_sem=recv, device_id=where, device_id_type=MESH)

    tensors = ((k_in, kbuf), (v_in, vbuf))

    def own_to(t, place, slot, other, side):
        src, buf = tensors[t]
        return remote(src.at[:, pl.ds(side * DIM, DIM)], buf.at[slot, half(core)],
                      kv_send.at[t, place * 2 + side], kv_recv.at[t, slot, core], device(other, side))

    def own_sends(t):
        for side in range(2):
            yield next_there, own_to(t, 1, 4, chip + 4, side)
            yield up_there, own_to(t, 0, 1, chip + 1, side)

    def to_sibling(t):
        src, buf = tensors[t]
        return remote(src.at[:, columns((1 - core) * DIM)], buf.at[0, half(core)],
                      kv_send.at[t, 4], kv_recv.at[t, 0, core], sibling)

    def heads_to_sibling(n):
        src, dst = ((q_in, qbuf), (g_in, gbuf))[n]
        for r in range(GROUP):
            yield remote(src.at[:, columns(((1 - core) * GROUP + r) * DIM)], dst.at[r, half(core)],
                         qg_send.at[n, r], qg_recv.at[n, r], sibling)

    def start_if(cond, copy):
        @pl.when(cond)
        def _():
            copy.start()

    for cond, copy in own_sends(0):
        start_if(cond, copy)
    to_sibling(0).start()
    for copy in heads_to_sibling(0):
        copy.start()
    for cond, copy in own_sends(1):
        start_if(cond, copy)
    to_sibling(1).start()
    for copy in heads_to_sibling(1):
        copy.start()

    position = chip * ROWS + lax.broadcasted_iota(jnp.int32, (1, ROWS), 1)

    def begins(n, first):
        edge = cu_ref[n]
        return jnp.where(edge <= position, edge, first)

    start_ref[...] = lax.fori_loop(0, cu_ref.shape[0], begins, jnp.zeros((1, ROWS), jnp.int32))
    m_ref[...] = jnp.full(m_ref.shape, HIDDEN, jnp.float32)
    l_ref[...] = jnp.zeros(l_ref.shape, jnp.float32)
    delta_ref[...] = jnp.zeros(delta_ref.shape, jnp.float32)
    dqt_ref[...] = jnp.zeros(dqt_ref.shape, jnp.float32)

    def arrived(t, slot, side):
        buf = tensors[t][1]
        view = buf.at[slot, half(side)]
        return remote(view, view, kv_send.at[t, 4], kv_recv.at[t, slot, side], sibling)

    def relay(t, slot, side):
        buf = tensors[t][1]
        below = from_below(slot)
        to = jnp.where(below, slot + 1, slot - 1)
        return remote(buf.at[slot, half(side)], buf.at[to, half(side)], relay_send.at[t, slot, side],
                      kv_recv.at[t, to, side], device(jnp.where(below, chip + 1, chip - 1), core))

    def take(t, slot):
        @pl.when(there(slot))
        def _():
            for side in range(2):
                arrived(t, slot, side).wait_recv()
                start_if(handed_on(slot), relay(t, slot, side))

    def units(slot, body):
        @pl.when(there(slot))
        def _():
            def step(n, carry):
                body(slot, n // GROUP, n % GROUP, slot * 2 * GROUP + n)
                return carry
            lax.fori_loop(0, 2 * GROUP, step, 0)

    def scores(slot, side, r, unit, diagonal=False):
        s = dot(kbuf[slot, half(side)], qbuf[r], NT) * TO_LOG2
        first = (chip - slot) * ROWS + side * TOK
        row = lax.broadcasted_iota(jnp.int32, s.shape, 0)
        seen = row >= start_ref[...] - first
        if diagonal:
            seen &= row + side * TOK <= lax.broadcasted_iota(jnp.int32, s.shape, 1)
        s = jnp.where(seen, s, HIDDEN)
        old = m_ref[r]
        new = jnp.maximum(old, jnp.max(s, axis=0, keepdims=True))
        e = jnp.exp2(s - new)
        l_ref[r] = l_ref[r] * jnp.exp2(old - new) + jnp.sum(e, axis=0, keepdims=True)
        m_ref[r] = new
        mu_ref[unit] = new
        e_ref[unit] = e

    def values(slot):
        @pl.when(there(slot))
        def _():
            for side in range(2):
                def step(r, acc):
                    unit = slot * 2 * GROUP + side * GROUP + r
                    p = e_ref[unit] * (jnp.exp2(mu_ref[unit] - m_ref[r]) * l_ref[r])
                    e_ref[unit] = p
                    return acc + dot(p.astype(jnp.bfloat16), gbuf[r])
                part_ref[1, slot, pl.ds(side * TOK, TOK)] = lax.fori_loop(
                    0, GROUP, step, jnp.zeros((TOK, DIM), jnp.float32))

    def prob_grads(slot, side, r, unit):
        d = dot(vbuf[slot, half(side)], gbuf[r], NT)
        d_ref[unit] = d
        delta_ref[r] += jnp.sum(e_ref[unit] * d, axis=0, keepdims=True)

    def keys(slot):
        @pl.when(there(slot))
        def _():
            for side in range(2):
                def step(r, acc):
                    unit = slot * 2 * GROUP + side * GROUP + r
                    ds = (e_ref[unit] * (d_ref[unit] - delta_ref[r])).astype(jnp.bfloat16)
                    dqt_ref[r] += dot(kbuf[slot, pl.ds(side * TOK, TOK)], ds, TN)
                    return acc + dot(ds, qbuf[r])
                part_ref[0, slot, pl.ds(side * TOK, TOK)] = SCALE * lax.fori_loop(
                    0, GROUP, step, jnp.zeros((TOK, DIM), jnp.float32))

    def back_arrived(t, index):
        view = back_ref.at[t, index]
        return remote(view, view, out_send.at[0], back_recv.at[t, index], sibling)

    def give(t, slot):
        below = from_below(slot)
        far = ~below & (slot == 4)
        index = jnp.where(below, slot - 1, jnp.where(far, 5, slot + 1))
        to = jnp.where(below, chip - 1, jnp.where(far, chip - 4, chip + 1))
        return remote(give_ref.at[t, slot], back_ref.at[t, index], back_send.at[t, slot],
                      back_recv.at[t, index], device(to, core))

    def send_back(t, slot):
        @pl.when(there(slot) & handed_on(slot))
        def _():
            back_arrived(t, slot).wait_recv()
            give_ref[t, slot] = (part_ref[t, slot] + back_ref[t, slot].astype(jnp.float32)).astype(jnp.bfloat16)

        @pl.when(there(slot) & ~handed_on(slot))
        def _():
            give_ref[t, slot] = part_ref[t, slot].astype(jnp.bfloat16)

        start_if(there(slot), give(t, slot))

    for n in list(range(GROUP)) + [2 * GROUP]:
        local[2 * n if n < GROUP else n].wait()
    arrived(0, 0, 1 - core).wait_recv()
    for copy in heads_to_sibling(0):
        copy.wait_recv()
    units(0, functools.partial(scores, diagonal=True))

    def key_step(place, carry):
        slot = arrival(place)
        take(0, slot)
        units(slot, scores)
        return carry

    lax.fori_loop(0, 4, key_step, 0)
    l_ref[...] = 1.0 / l_ref[...]

    for n in range(GROUP):
        local[2 * n + 1].wait()
    local[2 * GROUP + 1].wait()
    arrived(1, 0, 1 - core).wait_recv()
    for copy in heads_to_sibling(1):
        copy.wait_recv()

    def value_step(place, carry):
        take(1, arrival(place))
        slot = arrival(3 - place)
        values(slot)

        @pl.when(~handed_on(slot))
        def _():
            send_back(1, slot)
        return carry

    lax.fori_loop(0, 4, value_step, 0)
    values(0)

    units(0, prob_grads)

    def prob_step(place, carry):
        units(arrival(place), prob_grads)
        slot = arrival(3 - place)

        @pl.when(handed_on(slot))
        def _():
            send_back(1, slot)
        return carry

    lax.fori_loop(0, 4, prob_step, 0)

    def grad_step(place, carry):
        slot = arrival(3 - place)
        keys(slot)

        @pl.when(~handed_on(slot))
        def _():
            send_back(0, slot)
        return carry

    lax.fori_loop(0, 4, grad_step, 0)
    keys(0)

    for r in range(GROUP):
        dq_ref[:, r * DIM:(r + 1) * DIM] = (jnp.transpose(dqt_ref[r]) * SCALE).astype(jnp.bfloat16)
    wide = columns(core * GROUP * DIM, GROUP * DIM)
    dq_far = remote(dq_ref.at[half(1 - core)], dq_out.at[:, wide], out_send.at[0], out_recv.at[0], sibling)
    dq_far.start()
    dq_near = pltpu.make_async_copy(dq_ref.at[half(core)], dq_out.at[:, wide], local_sem.at[0])
    dq_near.start()

    def late_step(place, carry):
        slot = arrival(3 - place)

        @pl.when(handed_on(slot))
        def _():
            send_back(0, slot)
        return carry

    lax.fori_loop(0, 4, late_step, 0)

    copies = []
    for t, out in ((1, dv_out), (0, dk_out)):
        for is_there, index in ((up_there, 0), (next_there, 5)):
            @pl.when(is_there)
            def _(index=index):
                back_arrived(t, index).wait_recv()
                part_ref[t, 0] += back_ref[t, index].astype(jnp.float32)
        give_ref[t, 0] = part_ref[t, 0].astype(jnp.bfloat16)
        narrow = columns(core * DIM)
        far = remote(give_ref.at[t, 0, half(1 - core)], out.at[:, narrow], out_send.at[1 + t], out_recv.at[1 + t], sibling)
        near = pltpu.make_async_copy(give_ref.at[t, 0, half(core)], out.at[:, narrow], local_sem.at[1 + t])
        far.start()
        near.start()
        copies += [far, near]

    for t in range(2):
        for cond, copy in own_sends(t):
            @pl.when(cond)
            def _(copy=copy):
                copy.wait_send()
        to_sibling(t).wait_send()
        for copy in heads_to_sibling(t):
            copy.wait_send()
        for slot in range(1, 5):
            @pl.when(handed_on(slot))
            def _(slot=slot):
                for side in range(2):
                    relay(t, slot, side).wait_send()

            @pl.when(there(slot))
            def _(slot=slot):
                give(t, slot).wait_send()
    for copy in [dq_far, dq_near] + copies:
        copy.wait()


def per_device(query_states, key_states, value_states, out_grad, cu_seqlens):
    f32, bf16, i32 = jnp.float32, jnp.bfloat16, jnp.int32
    vmem, dma = pltpu.VMEM, pltpu.SemaphoreType.DMA
    anywhere = pl.BlockSpec(memory_space=pl.ANY)
    return pl.pallas_call(
        kernel,
        out_shape=(
            jax.ShapeDtypeStruct(query_states.shape, bf16),
            jax.ShapeDtypeStruct(key_states.shape, bf16),
            jax.ShapeDtypeStruct(value_states.shape, bf16),
        ),
        in_specs=[pl.BlockSpec(memory_space=pltpu.SMEM)] + [anywhere] * 4,
        out_specs=(anywhere,) * 3,
        scratch_shapes=[
            vmem((GROUP, ROWS, DIM), bf16), vmem((GROUP, ROWS, DIM), bf16),
            vmem((5, ROWS, DIM), bf16), vmem((5, ROWS, DIM), bf16),
            vmem((10 * GROUP, TOK, ROWS), f32), vmem((10 * GROUP, TOK, ROWS), f32),
            vmem((10 * GROUP, 1, ROWS), f32), vmem((GROUP, 1, ROWS), f32),
            vmem((GROUP, 1, ROWS), f32), vmem((GROUP, 1, ROWS), f32), vmem((1, ROWS), i32),
            vmem((2, 5, ROWS, DIM), f32), vmem((2, 6, ROWS, DIM), bf16), vmem((2, 5, ROWS, DIM), bf16),
            vmem((GROUP, DIM, ROWS), f32), vmem((ROWS, GROUP * DIM), bf16),
            dma((2 * GROUP + 2,)), dma((2, GROUP)), dma((2, GROUP)), dma((2, 5)), dma((2, 5, 2)), dma((2, 5, 2)),
            dma((2, 5)), dma((2, 6)), dma((3,)), dma((3,)),
        ],
        compiler_params=pltpu.CompilerParams(
            collective_id=0, has_side_effects=True, vmem_limit_bytes=60 << 20),
        name="attention_grads",
    )(cu_seqlens, query_states, key_states, value_states, out_grad)


def solution(mesh):
    split = P(("dp", "outer", "inner"), None)
    return jax.shard_map(
        per_device,
        mesh=mesh,
        in_specs=(split, split, split, split, P("dp")),
        out_specs=(split, split, split),
        check_vma=False,
    )
```

time: 318 us -> 94.2 us (0.30)
  the two profiles are of different devices: /device:TPU:62 before, /device:TPU:7 now
where the time goes in v1:
time: 94.2 us; the launch traced here: 94 us
  Pallas kernels  89.9 us (95%)
  local copies, waits for them, and re-layouts  3.51 us (4%)
    pallas_call x1, Pallas kernels, per_device(): pl.pallas_call(kernel, out_shape=(jax.ShapeDtypeStruct(query_states.shape...  89.9 us
    unnamed x7, local copies, waits for them, and re-layouts  3.51 us

profile of v1, /device:TPU:7, one launch (start us, length us, event | category | flops | bytes accessed | tf_op | source)
XLA Modules:
  0.0 94.0 jit_solution(18194044391418750933)
XLA Ops:
  0.6 89.9 %attention_grads.1 = (bf16[256,1024]{1,0:T(8,128)(2,1)}, bf16[256,256]{1,0:T(8,128)(2,1)}, bf16[256,256]{1,0:T(8,128)(2,1)}) custom-call(s32[65]{0:T(128)} %cu_ref.1, bf16[256,1024]{1,0:T(8,128)(2,1)} %q_in.1, bf16[256,256]{1,0:T(8,128)(2,1)} %k_in.1, bf16[256,256]{1,0:T(8,128)(2,1)} %v_in.1, bf16[256,1024]{1,0:T(8,128)(2,1)} %g_in.1), custom_call_target="tpu_custom_call" | custom-call | tf_op jit(solution)/shard_map/attention_grads/pallas_call | solution.py:369
  90.5 0.0 copy-start.1
  90.5 1.9 %copy.11 = bf16[256,1024]{1,0:T(8,128)(2,1)} copy(bf16[256,1024]{1,0:T(8,128)(2,1)} %get-tuple-element.6) | data formatting | bytes 1048576
  92.4 0.0 copy-done.1
  92.4 0.0 copy-start
  92.4 0.7 copy.12
  93.1 0.3 copy-done
  93.4 0.7 copy.13
Async XLA Ops:
  90.5 1.9 %copy-start.1 = (bf16[256,256]{1,0:T(8,128)(2,1)S(1)}, bf16[256,256]{1,0:T(8,128)(2,1)}, u32[]{:S(2)}) copy-start(bf16[256,256]{1,0:T(8,128)(2,1)} %get-tuple-element.7) | copy-start | bytes 393220
  92.4 1.0 %copy-start = (bf16[256,256]{1,0:T(8,128)(2,1)S(1)}, bf16[256,256]{1,0:T(8,128)(2,1)}, u32[]{:S(2)}) copy-start(bf16[256,256]{1,0:T(8,128)(2,1)} %get-tuple-element.8) | copy-start | bytes 393220

commit v2 on v1

--- a/solution.py
+++ b/solution.py
@@ -18,13 +18,16 @@
 NT = (((1,), (1,)), ((), ()))
 TN = (((0,), (0,)), ((), ()))
 
-ORDERS = ((4, 3, 2, 1), (4, 1, 3, 2), (1, 4, 2, 3), (1, 2, 3, 4))
-PACKED = sum(
-    (distance - 1) * 4 ** (4 * row + 3 - place)
-    for row, order in enumerate(ORDERS)
-    for place, distance in enumerate(order)
-)
-LAG = 2
+def packed(orders):
+    return sum(
+        (distance - 1) * 4 ** (4 * row + 3 - place)
+        for row, order in enumerate(orders)
+        for place, distance in enumerate(order)
+    )
+
+
+TAKEN = packed(((4, 3, 2, 1), (2, 4, 1, 3), (2, 1, 4, 3)))
+TAKEN_LAST = packed(((1, 2, 4, 3), (1, 2, 3, 4)))
 
 
 def dot(a, b, dims=(((1,), (0,)), ((), ()))):
@@ -43,29 +46,42 @@
     z = inner // 2
     chip = outer * 4 + z
     fold = outer == 4
-    up_there = (z < 3) | (outer == 3)
-    down_there = (z > 0) | fold
-    next_there = (outer != 3) & (outer != 7)
-    last_there = (outer != 0) & (outer != 4)
+    ahead, behind = jnp.minimum(4, 31 - chip), jnp.minimum(4, chip)
+    edge = (outer == 3) & (z == 3)
+    chain = fold | edge
 
     def device(which, side):
         return {"outer": which // 4, "inner": (which % 4) * 2 + side}
 
     sibling = device(chip, 1 - core)
 
-    def from_below(slot):
-        return (slot <= z) | fold
+    def sent(d):
+        if d == 1:
+            return (z < 3) | edge
+        within = (z + d <= 3) & ~fold
+        if d == 3:
+            within &= z > 0
+        return within | ((z + d > 3) & (outer != 3) & (outer != 7))
 
     def there(slot):
         return (slot <= z) | (outer != 0)
 
+    def goes_down(slot):
+        return (z == 1) & (slot == 2) & ~fold & (outer != 0)
+
+    def goes_up(slot):
+        return (slot < 4) & ((fold & (z < 3)) | edge) | ((z == 2) & (slot == 2) & ~fold)
+
     def handed_on(slot):
-        below = from_below(slot)
-        return there(slot) & ((below & (slot < 4) & up_there) | (~below & (z > 0)))
-
-    def arrival(place):
-        row = jnp.where(fold, 3, jnp.minimum(z, 2))
-        digits = PACKED // jnp.where(row == 0, 1, jnp.where(row == 1, 4**4, jnp.where(row == 2, 4**8, 4**12)))
+        return goes_up(slot) | goes_down(slot)
+
+    def has_child(slot):
+        return (slot < 4) & ((fold & (z < 3)) | edge)
+
+    def order(place):
+        last = jnp.where((z == 3) | fold, 1, 0)
+        row = jnp.where(last == 1, jnp.where(chain, 1, 0), z)
+        digits = jnp.where(last == 1, TAKEN_LAST, TAKEN) // jnp.where(row == 0, 1, jnp.where(row == 1, 4**4, 4**8))
         power = jnp.where(place == 0, 64, jnp.where(place == 1, 16, jnp.where(place == 2, 4, 1)))
         return (digits // power) % 4 + 1
 
@@ -88,13 +104,13 @@
 
     barrier = pltpu.get_barrier_semaphore()
     pl.semaphore_signal(barrier, 1, device_id=sibling, device_id_type=MESH)
-    for is_there, other in ((up_there, chip + 1), (down_there, chip - 1), (next_there, chip + 4), (last_there, chip - 4)):
-        @pl.when(is_there)
-        def _(other=other):
-            for side in range(2):
-                pl.semaphore_signal(barrier, 1, device_id=device(other, side), device_id_type=MESH)
-    pl.semaphore_wait(barrier, 1 + 2 * sum(
-        jnp.where(is_there, 1, 0) for is_there in (up_there, down_there, next_there, last_there)))
+    for d in range(1, 5):
+        for is_there, other in ((d <= ahead, chip + d), (d <= behind, chip - d)):
+            @pl.when(is_there)
+            def _(other=other):
+                for side in range(2):
+                    pl.semaphore_signal(barrier, 1, device_id=device(other, side), device_id_type=MESH)
+    pl.semaphore_wait(barrier, 1 + 2 * (ahead + behind))
 
     def remote(src, dst, send, recv, where):
         return pltpu.make_async_remote_copy(
@@ -102,20 +118,18 @@
 
     tensors = ((k_in, kbuf), (v_in, vbuf))
 
-    def own_to(t, place, slot, other, side):
+    def own_sends(t):
         src, buf = tensors[t]
-        return remote(src.at[:, pl.ds(side * DIM, DIM)], buf.at[slot, half(core)],
-                      kv_send.at[t, place * 2 + side], kv_recv.at[t, slot, core], device(other, side))
-
-    def own_sends(t):
-        for side in range(2):
-            yield next_there, own_to(t, 1, 4, chip + 4, side)
-            yield up_there, own_to(t, 0, 1, chip + 1, side)
+        for n, d in enumerate((2, 1, 3, 4)):
+            for side in range(2):
+                yield sent(d), remote(
+                    src.at[:, pl.ds(side * DIM, DIM)], buf.at[d, half(core)], kv_send.at[t, 2 * n + side],
+                    kv_recv.at[t, d, core], device(chip + d, side))
 
     def to_sibling(t):
         src, buf = tensors[t]
         return remote(src.at[:, columns((1 - core) * DIM)], buf.at[0, half(core)],
-                      kv_send.at[t, 4], kv_recv.at[t, 0, core], sibling)
+                      kv_send.at[t, 8], kv_recv.at[t, 0, core], sibling)
 
     def heads_to_sibling(n):
         src, dst = ((q_in, qbuf), (g_in, gbuf))[n]
@@ -133,8 +147,6 @@
     to_sibling(0).start()
     for copy in heads_to_sibling(0):
         copy.start()
-    for cond, copy in own_sends(1):
-        start_if(cond, copy)
     to_sibling(1).start()
     for copy in heads_to_sibling(1):
         copy.start()
@@ -154,14 +166,14 @@
     def arrived(t, slot, side):
         buf = tensors[t][1]
         view = buf.at[slot, half(side)]
-        return remote(view, view, kv_send.at[t, 4], kv_recv.at[t, slot, side], sibling)
+        return remote(view, view, kv_send.at[t, 8], kv_recv.at[t, slot, side], sibling)
 
     def relay(t, slot, side):
         buf = tensors[t][1]
-        below = from_below(slot)
-        to = jnp.where(below, slot + 1, slot - 1)
+        down = goes_down(slot)
+        to = jnp.where(down, slot - 1, slot + 1)
         return remote(buf.at[slot, half(side)], buf.at[to, half(side)], relay_send.at[t, slot, side],
-                      kv_recv.at[t, to, side], device(jnp.where(below, chip + 1, chip - 1), core))
+                      kv_recv.at[t, to, side], device(jnp.where(down, chip - 1, chip + 1), core))
 
     def take(t, slot):
         @pl.when(there(slot))
@@ -176,7 +188,7 @@
             def step(n, carry):
                 body(slot, n // GROUP, n % GROUP, slot * 2 * GROUP + n)
                 return carry
-            lax.fori_loop(0, 2 * GROUP, step, 0)
+            lax.fori_loop(0, 2 * GROUP, step, 0, unroll=True)
 
     def scores(slot, side, r, unit, diagonal=False):
         s = dot(kbuf[slot, half(side)], qbuf[r], NT) * TO_LOG2
@@ -204,7 +216,7 @@
                     e_ref[unit] = p
                     return acc + dot(p.astype(jnp.bfloat16), gbuf[r])
                 part_ref[1, slot, pl.ds(side * TOK, TOK)] = lax.fori_loop(
-                    0, GROUP, step, jnp.zeros((TOK, DIM), jnp.float32))
+                    0, GROUP, step, jnp.zeros((TOK, DIM), jnp.float32), unroll=True)
 
     def prob_grads(slot, side, r, unit):
         d = dot(vbuf[slot, half(side)], gbuf[r], NT)
@@ -221,31 +233,32 @@
                     dqt_ref[r] += dot(kbuf[slot, pl.ds(side * TOK, TOK)], ds, TN)
                     return acc + dot(ds, qbuf[r])
                 part_ref[0, slot, pl.ds(side * TOK, TOK)] = SCALE * lax.fori_loop(
-                    0, GROUP, step, jnp.zeros((TOK, DIM), jnp.float32))
+                    0, GROUP, step, jnp.zeros((TOK, DIM), jnp.float32), unroll=True)
 
     def back_arrived(t, index):
         view = back_ref.at[t, index]
         return remote(view, view, out_send.at[0], back_recv.at[t, index], sibling)
 
     def give(t, slot):
-        below = from_below(slot)
-        far = ~below & (slot == 4)
-        index = jnp.where(below, slot - 1, jnp.where(far, 5, slot + 1))
-        to = jnp.where(below, chip - 1, jnp.where(far, chip - 4, chip + 1))
+        index = jnp.where(fold, slot + 3, slot - 1)
+        to = jnp.where(fold, chip - 1, chip - slot)
         return remote(give_ref.at[t, slot], back_ref.at[t, index], back_send.at[t, slot],
                       back_recv.at[t, index], device(to, core))
 
     def send_back(t, slot):
-        @pl.when(there(slot) & handed_on(slot))
-        def _():
-            back_arrived(t, slot).wait_recv()
-            give_ref[t, slot] = (part_ref[t, slot] + back_ref[t, slot].astype(jnp.float32)).astype(jnp.bfloat16)
-
-        @pl.when(there(slot) & ~handed_on(slot))
+        @pl.when(there(slot) & has_child(slot))
+        def _():
+            back_arrived(t, slot + 4).wait_recv()
+            give_ref[t, slot] = (part_ref[t, slot] + back_ref[t, slot + 4].astype(jnp.float32)).astype(jnp.bfloat16)
+
+        @pl.when(there(slot) & ~has_child(slot))
         def _():
             give_ref[t, slot] = part_ref[t, slot].astype(jnp.bfloat16)
 
         start_if(there(slot), give(t, slot))
+
+    def given(d):
+        return jnp.where(z + d <= 3, outer != 4, (outer != 3) & (outer != 7))
 
     for n in list(range(GROUP)) + [2 * GROUP]:
         local[2 * n if n < GROUP else n].wait()
@@ -255,8 +268,13 @@
     units(0, functools.partial(scores, diagonal=True))
 
     def key_step(place, carry):
-        slot = arrival(place)
+        slot = order(place)
         take(0, slot)
+
+        @pl.when(place == jnp.where(chain, 3, 0))
+        def _():
+            for cond, copy in own_sends(1):
+                start_if(cond, copy)
         units(slot, scores)
         return carry
 
@@ -271,11 +289,11 @@
         copy.wait_recv()
 
     def value_step(place, carry):
-        take(1, arrival(place))
-        slot = arrival(3 - place)
+        take(1, order(place))
+        slot = order(3 - place)
         values(slot)
 
-        @pl.when(~handed_on(slot))
+        @pl.when(~has_child(slot))
         def _():
             send_back(1, slot)
         return carry
@@ -286,10 +304,10 @@
     units(0, prob_grads)
 
     def prob_step(place, carry):
-        units(arrival(place), prob_grads)
-        slot = arrival(3 - place)
-
-        @pl.when(handed_on(slot))
+        units(order(place), prob_grads)
+        slot = order(3 - place)
+
+        @pl.when(has_child(slot))
         def _():
             send_back(1, slot)
         return carry
@@ -297,10 +315,10 @@
     lax.fori_loop(0, 4, prob_step, 0)
 
     def grad_step(place, carry):
-        slot = arrival(3 - place)
+        slot = order(3 - place)
         keys(slot)
 
-        @pl.when(~handed_on(slot))
+        @pl.when(~has_child(slot))
         def _():
             send_back(0, slot)
         return carry
@@ -317,9 +335,9 @@
     dq_near.start()
 
     def late_step(place, carry):
-        slot = arrival(3 - place)
-
-        @pl.when(handed_on(slot))
+        slot = order(3 - place)
+
+        @pl.when(has_child(slot))
         def _():
             send_back(0, slot)
         return carry
@@ -328,7 +346,7 @@
 
     copies = []
     for t, out in ((1, dv_out), (0, dk_out)):
-        for is_there, index in ((up_there, 0), (next_there, 5)):
+        for is_there, index in [(given(d), d - 1) for d in range(1, 5)] + [(has_child(0), 4)]:
             @pl.when(is_there)
             def _(index=index):
                 back_arrived(t, index).wait_recv()
@@ -381,10 +399,10 @@
             vmem((10 * GROUP, TOK, ROWS), f32), vmem((10 * GROUP, TOK, ROWS), f32),
             vmem((10 * GROUP, 1, ROWS), f32), vmem((GROUP, 1, ROWS), f32),
             vmem((GROUP, 1, ROWS), f32), vmem((GROUP, 1, ROWS), f32), vmem((1, ROWS), i32),
-            vmem((2, 5, ROWS, DIM), f32), vmem((2, 6, ROWS, DIM), bf16), vmem((2, 5, ROWS, DIM), bf16),
+            vmem((2, 5, ROWS, DIM), f32), vmem((2, 8, ROWS, DIM), bf16), vmem((2, 5, ROWS, DIM), bf16),
             vmem((GROUP, DIM, ROWS), f32), vmem((ROWS, GROUP * DIM), bf16),
-            dma((2 * GROUP + 2,)), dma((2, GROUP)), dma((2, GROUP)), dma((2, 5)), dma((2, 5, 2)), dma((2, 5, 2)),
-            dma((2, 5)), dma((2, 6)), dma((3,)), dma((3,)),
+            dma((2 * GROUP + 2,)), dma((2, GROUP)), dma((2, GROUP)), dma((2, 9)), dma((2, 5, 2)), dma((2, 5, 2)),
+            dma((2, 5)), dma((2, 8)), dma((3,)), dma((3,)),
         ],
         compiler_params=pltpu.CompilerParams(
             collective_id=0, has_side_effects=True, vmem_limit_bytes=60 << 20),

time: 94.2 us -> 79.5 us (0.84)
  the two profiles are of different devices: /device:TPU:7 before, /device:TPU:87 now
where the time goes in v2:
time: 79.5 us; the launch traced here: 79.4 us
  Pallas kernels  75.2 us (95%)
  local copies, waits for them, and re-layouts  3.51 us (4%)
    pallas_call x1, Pallas kernels, per_device(): pl.pallas_call(kernel, out_shape=(jax.ShapeDtypeStruct(query_states.shape...  75.2 us
    unnamed x7, local copies, waits for them, and re-layouts  3.51 us

profile of v2, /device:TPU:87, one launch (start us, length us, event | category | flops | bytes accessed | tf_op | source)
XLA Modules:
  0.0 79.4 jit_solution(18185097096973392270)
XLA Ops:
  0.6 75.2 %attention_grads.1 = (bf16[256,1024]{1,0:T(8,128)(2,1)}, bf16[256,256]{1,0:T(8,128)(2,1)}, bf16[256,256]{1,0:T(8,128)(2,1)}) custom-call(s32[65]{0:T(128)} %cu_ref.1, bf16[256,1024]{1,0:T(8,128)(2,1)} %q_in.1, bf16[256,256]{1,0:T(8,128)(2,1)} %k_in.1, bf16[256,256]{1,0:T(8,128)(2,1)} %v_in.1, bf16[256,1024]{1,0:T(8,128)(2,1)} %g_in.1), custom_call_target="tpu_custom_call" | custom-call | tf_op jit(solution)/shard_map/attention_grads/pallas_call | solution.py:387
  75.9 0.0 copy-start.1
  75.9 1.9 %copy.11 = bf16[256,1024]{1,0:T(8,128)(2,1)} copy(bf16[256,1024]{1,0:T(8,128)(2,1)} %get-tuple-element.6) | data formatting | bytes 1048576
  77.8 0.0 copy-done.1
  77.8 0.0 copy-start
  77.8 0.7 copy.12
  78.4 0.3 copy-done
  78.7 0.7 copy.13
Async XLA Ops:
  75.9 1.9 %copy-start.1 = (bf16[256,256]{1,0:T(8,128)(2,1)S(1)}, bf16[256,256]{1,0:T(8,128)(2,1)}, u32[]{:S(2)}) copy-start(bf16[256,256]{1,0:T(8,128)(2,1)} %get-tuple-element.7) | copy-start | bytes 393220
  77.8 1.0 %copy-start = (bf16[256,256]{1,0:T(8,128)(2,1)S(1)}, bf16[256,256]{1,0:T(8,128)(2,1)}, u32[]{:S(2)}) copy-start(bf16[256,256]{1,0:T(8,128)(2,1)} %get-tuple-element.8) | copy-start | bytes 393220

commit v3 on v2

--- a/solution.py
+++ b/solution.py
@@ -27,6 +27,7 @@
 
 
 TAKEN = packed(((4, 3, 2, 1), (2, 4, 1, 3), (2, 1, 4, 3)))
+BACK_FOLD = packed(((3, 4, 1, 2), (4, 3, 2, 1), (4, 2, 1, 3), (2, 3, 4, 1)))
 TAKEN_LAST = packed(((1, 2, 4, 3), (1, 2, 3, 4)))
 
 
@@ -40,6 +41,7 @@
     qbuf, gbuf, kbuf, vbuf, e_ref, d_ref, mu_ref, m_ref, l_ref, delta_ref, start_ref,
     part_ref, back_ref, give_ref, dqt_ref, dq_ref,
     local_sem, qg_send, qg_recv, kv_send, kv_recv, relay_send, back_send, back_recv, out_send, out_recv,
+    hub_ref, hub_recv, hub_send, hub_back_send,
 ):
     outer, inner = lax.axis_index("outer"), lax.axis_index("inner")
     core = inner % 2
@@ -48,7 +50,17 @@
     fold = outer == 4
     ahead, behind = jnp.minimum(4, 31 - chip), jnp.minimum(4, chip)
     edge = (outer == 3) & (z == 3)
-    chain = fold | edge
+    chain = edge | fold
+    head = fold & (z == 0)
+    met = (
+        (chip == 12, ((18, core), (19, core))),
+        (fold & (z > 1), ((12, core),)),
+        (chip == 0, ((14, core), (15, core), (18, core), (19, core))),
+        (((outer == 3) | fold) & (z > 1), ((0, core),)),
+        (chip == 3, ((15, 0), (15, 1), (16, core))),
+        (edge, ((3, 0), (3, 1))),
+        (head, ((3, core),)),
+    )
 
     def device(which, side):
         return {"outer": which // 4, "inner": (which % 4) * 2 + side}
@@ -57,7 +69,9 @@
 
     def sent(d):
         if d == 1:
-            return (z < 3) | edge
+            return z < 3
+        if d == 2:
+            return ((z < 2) & ~fold) | edge | ((z > 1) & (outer != 3) & (outer != 7))
         within = (z + d <= 3) & ~fold
         if d == 3:
             within &= z > 0
@@ -70,20 +84,34 @@
         return (z == 1) & (slot == 2) & ~fold & (outer != 0)
 
     def goes_up(slot):
-        return (slot < 4) & ((fold & (z < 3)) | edge) | ((z == 2) & (slot == 2) & ~fold)
+        return (
+            (edge & (slot < 4)) | (head & ((slot == 2) | (slot == 3)))
+            | (fold & (z == 1) & ((slot == 1) | (slot == 3))) | (fold & (z == 2) & (slot < 3))
+            | ((z == 2) & (slot == 2))
+        )
 
     def handed_on(slot):
         return goes_up(slot) | goes_down(slot)
 
     def has_child(slot):
-        return (slot < 4) & ((fold & (z < 3)) | edge)
+        across = (edge & (slot < 4)) | (fold & (z == 2) & (slot > 2))
+        return across | (head & (slot == 3)) | ((slot == 2) & (((z == 2) & (outer != 3)) | ((z == 1) & ~fold & (outer != 0))))
+
+    def deferred(slot):
+        return (edge & (slot < 4)) | (fold & (z == 2) & (slot > 2))
 
     def order(place):
-        last = jnp.where((z == 3) | fold, 1, 0)
+        last = jnp.where((z == 3) | chain, 1, 0)
         row = jnp.where(last == 1, jnp.where(chain, 1, 0), z)
-        digits = jnp.where(last == 1, TAKEN_LAST, TAKEN) // jnp.where(row == 0, 1, jnp.where(row == 1, 4**4, 4**8))
+        return digit(jnp.where(last == 1, TAKEN_LAST, TAKEN), row, place)
+
+    def digit(table, row, place):
+        digits = table // jnp.where(row == 0, 1, jnp.where(row == 1, 4**4, jnp.where(row == 2, 4**8, 4**12)))
         power = jnp.where(place == 0, 64, jnp.where(place == 1, 16, jnp.where(place == 2, 4, 1)))
         return (digits // power) % 4 + 1
+
+    def back_order(place):
+        return jnp.where(fold, digit(BACK_FOLD, (z + 2) % 4, place), order(3 - place))
 
     def half(side):
         return pl.ds(pl.multiple_of(side * TOK, TOK), TOK)
@@ -110,7 +138,15 @@
             def _(other=other):
                 for side in range(2):
                     pl.semaphore_signal(barrier, 1, device_id=device(other, side), device_id_type=MESH)
-    pl.semaphore_wait(barrier, 1 + 2 * (ahead + behind))
+    met_count = 0
+    for is_there, others in met:
+        met_count += jnp.where(is_there, len(others), 0)
+
+        @pl.when(is_there)
+        def _(others=others):
+            for other in others:
+                pl.semaphore_signal(barrier, 1, device_id=device(*other), device_id_type=MESH)
+    pl.semaphore_wait(barrier, 1 + 2 * (ahead + behind) + met_count)
 
     def remote(src, dst, send, recv, where):
         return pltpu.make_async_remote_copy(
@@ -125,6 +161,48 @@
                 yield sent(d), remote(
                     src.at[:, pl.ds(side * DIM, DIM)], buf.at[d, half(core)], kv_send.at[t, 2 * n + side],
                     kv_recv.at[t, d, core], device(chip + d, side))
+
+    def own_hub_sends(t):
+        src, buf = tensors[t]
+        for side in range(2):
+            yield edge, remote(
+                src.at[:, pl.ds(side * DIM, DIM)], hub_ref.at[t, 0, half(core)], kv_send.at[t, 9 + side],
+                hub_recv.at[t, 0, core], device(12, side))
+        yield edge, remote(
+            src.at[:, pl.ds(0, DIM)], buf.at[1, half(core)], kv_send.at[t, 11],
+            kv_recv.at[t, 1, core], device(16, 0))
+        yield edge, remote(
+            src.at[:, pl.ds(DIM, DIM)], hub_ref.at[t, 1, half(core)], kv_send.at[t, 12],
+            hub_recv.at[t, 1, core], device(3, 1))
+
+    def hub_arrived(t, n, side):
+        view = hub_ref.at[t, n, half(side)]
+        return remote(view, view, kv_send.at[t, 8], hub_recv.at[t, n, side], sibling)
+
+    def hub_sends(t, side):
+        for k, (to, slot) in enumerate(((19, 4), (18, 3))):
+            yield remote(hub_ref.at[t, 0, half(side)], tensors[t][1].at[slot, half(side)], hub_send.at[t, k, side],
+                         kv_recv.at[t, slot, side], device(to, core))
+
+    def round_send(t, slot, side):
+        return remote(hub_ref.at[t, slot, half(side)], tensors[t][1].at[slot, half(side)], hub_send.at[t, slot - 1, side],
+                      kv_recv.at[t, slot, side], device(16, core))
+
+    def hub(t):
+        @pl.when(chip == 12)
+        def _():
+            for side in range(2):
+                hub_arrived(t, 0, side).wait_recv()
+                for copy in hub_sends(t, side):
+                    copy.start()
+
+    def hub_round(t, slots):
+        @pl.when((chip == 3) & (core == 1))
+        def _():
+            for slot in slots:
+                for side in range(2):
+                    hub_arrived(t, slot, side).wait_recv()
+                    round_send(t, slot, side).start()
 
     def to_sibling(t):
         src, buf = tensors[t]
@@ -142,7 +220,7 @@
         def _():
             copy.start()
 
-    for cond, copy in own_sends(0):
+    for cond, copy in list(own_hub_sends(0)) + list(own_sends(0)):
         start_if(cond, copy)
     to_sibling(0).start()
     for copy in heads_to_sibling(0):
@@ -180,7 +258,13 @@
         def _():
             for side in range(2):
                 arrived(t, slot, side).wait_recv()
-                start_if(handed_on(slot), relay(t, slot, side))
+                wide = edge & (core == 1)
+                start_if(handed_on(slot) & ~wide, relay(t, slot, side))
+
+                @pl.when(handed_on(slot) & wide)
+                def _():
+                    remote(tensors[t][1].at[slot, half(side)], hub_ref.at[t, slot + 1, half(side)],
+                           relay_send.at[t, slot, side], hub_recv.at[t, slot + 1, side], device(3, core)).start()
 
     def units(slot, body):
         @pl.when(there(slot))
@@ -206,14 +290,16 @@
         mu_ref[unit] = new
         e_ref[unit] = e
 
+    def share(unit, r):
+        return jnp.exp2(mu_ref[unit] - m_ref[r]) * l_ref[r]
+
     def values(slot):
         @pl.when(there(slot))
         def _():
             for side in range(2):
                 def step(r, acc):
                     unit = slot * 2 * GROUP + side * GROUP + r
-                    p = e_ref[unit] * (jnp.exp2(mu_ref[unit] - m_ref[r]) * l_ref[r])
-                    e_ref[unit] = p
+                    p = e_ref[unit] * share(unit, r)
                     return acc + dot(p.astype(jnp.bfloat16), gbuf[r])
                 part_ref[1, slot, pl.ds(side * TOK, TOK)] = lax.fori_loop(
                     0, GROUP, step, jnp.zeros((TOK, DIM), jnp.float32), unroll=True)
@@ -221,7 +307,7 @@
     def prob_grads(slot, side, r, unit):
         d = dot(vbuf[slot, half(side)], gbuf[r], NT)
         d_ref[unit] = d
-        delta_ref[r] += jnp.sum(e_ref[unit] * d, axis=0, keepdims=True)
+        delta_ref[r] += jnp.sum(e_ref[unit] * d, axis=0, keepdims=True) * share(unit, r)
 
     def keys(slot):
         @pl.when(there(slot))
@@ -229,36 +315,73 @@
             for side in range(2):
                 def step(r, acc):
                     unit = slot * 2 * GROUP + side * GROUP + r
-                    ds = (e_ref[unit] * (d_ref[unit] - delta_ref[r])).astype(jnp.bfloat16)
+                    ds = (e_ref[unit] * share(unit, r) * (d_ref[unit] - delta_ref[r])).astype(jnp.bfloat16)
                     dqt_ref[r] += dot(kbuf[slot, pl.ds(side * TOK, TOK)], ds, TN)
                     return acc + dot(ds, qbuf[r])
                 part_ref[0, slot, pl.ds(side * TOK, TOK)] = SCALE * lax.fori_loop(
                     0, GROUP, step, jnp.zeros((TOK, DIM), jnp.float32), unroll=True)
 
-    def back_arrived(t, index):
-        view = back_ref.at[t, index]
-        return remote(view, view, out_send.at[0], back_recv.at[t, index], sibling)
-
-    def give(t, slot):
-        index = jnp.where(fold, slot + 3, slot - 1)
-        to = jnp.where(fold, chip - 1, chip - slot)
-        return remote(give_ref.at[t, slot], back_ref.at[t, index], back_send.at[t, slot],
-                      back_recv.at[t, index], device(to, core))
+    def back_arrived(t, index, side):
+        view = back_ref.at[t, index, half(side)]
+        return remote(view, view, out_send.at[0], back_recv.at[t, index, side], sibling)
+
+    def give(t, slot, side):
+        over = fold & (slot > z)
+        index = jnp.where(z == 0, slot + 3, jnp.where(
+            z == 1, jnp.where(slot == 4, 7, slot + 5), jnp.where(z == 2, 10 - slot, 4)))
+        index = jnp.where(over, index, slot - 1)
+        to = jnp.where(z == 0, 15, jnp.where(z == 1, jnp.where(slot == 4, 16, 18), 0))
+        to = jnp.where(over, to, chip - slot)
+        down = (z == 3) & (slot == 3) & ~edge
+        up = (z == 0) & (slot == 1) & ~fold
+        index = jnp.where(down | up, 6, index)
+        to = jnp.where(down, chip - 1, jnp.where(up, chip + 1, to))
+        return remote(give_ref.at[t, slot, half(side)], back_ref.at[t, index, half(side)],
+                      back_send.at[t, slot, side], back_recv.at[t, index, side], device(to, core))
 
     def send_back(t, slot):
-        @pl.when(there(slot) & has_child(slot))
-        def _():
-            back_arrived(t, slot + 4).wait_recv()
-            give_ref[t, slot] = (part_ref[t, slot] + back_ref[t, slot + 4].astype(jnp.float32)).astype(jnp.bfloat16)
-
-        @pl.when(there(slot) & ~has_child(slot))
-        def _():
-            give_ref[t, slot] = part_ref[t, slot].astype(jnp.bfloat16)
-
-        start_if(there(slot), give(t, slot))
+        @pl.when(there(slot))
+        def _():
+            for side in range(2):
+                rows = half(side)
+
+                @pl.when(has_child(slot))
+                def _():
+                    back_arrived(t, slot + 4, side).wait_recv()
+                    part_ref[t, slot, rows] += back_ref[t, slot + 4, rows].astype(jnp.float32)
+
+                give_ref[t, slot, rows] = part_ref[t, slot, rows].astype(jnp.bfloat16)
+                give(t, slot, side).start()
 
     def given(d):
-        return jnp.where(z + d <= 3, outer != 4, (outer != 3) & (outer != 7))
+        across = (z + d > 3) & (outer != 3) & (outer != 7)
+        if d == 1:
+            return (z < 3) | (across & (z < 3))
+        if d == 3:
+            return ((z == 0) & (outer == 3)) | across
+        return (z + d <= 3) | across
+
+    def hub_back_sends(t, side):
+        rows = half(side)
+        for k, src in enumerate((back_ref.at[t, 6, rows], give_ref.at[t, 1, rows])):
+            yield remote(src, back_ref.at[t, 8, rows], hub_back_send.at[t, k, side],
+                         back_recv.at[t, 8, side], device(14 + k, core))
+
+    def hub_back(t):
+        @pl.when(chip == 0)
+        def _():
+            for side in range(2):
+                rows = half(side)
+                _, summed = hub_back_sends(t, side)
+                back_arrived(t, 4, side).wait_recv()
+                back_arrived(t, 7, side).wait_recv()
+                both = back_ref[t, 4, rows].astype(jnp.float32) + back_ref[t, 7, rows].astype(jnp.float32)
+                give_ref[t, 1, rows] = both.astype(jnp.bfloat16)
+                summed.start()
+            for side in range(2):
+                straight, _ = hub_back_sends(t, side)
+                back_arrived(t, 6, side).wait_recv()
+                straight.start()
 
     for n in list(range(GROUP)) + [2 * GROUP]:
         local[2 * n if n < GROUP else n].wait()
@@ -269,12 +392,29 @@
 
     def key_step(place, carry):
         slot = order(place)
+
+        @pl.when(place == 0)
+        def _():
+            hub(0)
+            hub_round(0, (1, 2, 3, 4))
+
         take(0, slot)
 
-        @pl.when(place == jnp.where(chain, 3, 0))
-        def _():
-            for cond, copy in own_sends(1):
+        @pl.when(place == 0)
+        def _():
+            for cond, copy in list(own_hub_sends(1)) + list(own_sends(1)):
                 start_if(cond, copy)
+
+        @pl.when(place == 1)
+        def _():
+            hub_round(1, (1, 2))
+
+        @pl.when(place == 3)
+        def _():
+            hub(1)
+            hub_round(1, (3, 4))
+            take(1, order(0))
+
         units(slot, scores)
         return carry
 
@@ -288,43 +428,56 @@
     for copy in heads_to_sibling(1):
         copy.wait_recv()
 
+    units(0, prob_grads)
+
     def value_step(place, carry):
-        take(1, order(place))
-        slot = order(3 - place)
+        slot = back_order(place)
         values(slot)
 
-        @pl.when(~has_child(slot))
+        @pl.when(~deferred(slot))
         def _():
             send_back(1, slot)
+
+        units(order(place), prob_grads)
+
+        @pl.when(place < 3)
+        def _():
+            take(1, order(place + 1))
+
+        before = back_order(place - 2)
+
+        @pl.when((place > 1) & deferred(before))
+        def _():
+            send_back(1, before)
         return carry
 
     lax.fori_loop(0, 4, value_step, 0)
     values(0)
-
-    units(0, prob_grads)
-
-    def prob_step(place, carry):
-        units(order(place), prob_grads)
-        slot = order(3 - place)
-
-        @pl.when(has_child(slot))
-        def _():
-            send_back(1, slot)
-        return carry
-
-    lax.fori_loop(0, 4, prob_step, 0)
+    hub_back(1)
 
     def grad_step(place, carry):
-        slot = order(3 - place)
+        slot = back_order(place)
         keys(slot)
-
-        @pl.when(~has_child(slot))
+        early = back_order(place + 2)
+
+        @pl.when((place < 2) & deferred(early))
+        def _():
+            send_back(1, early)
+
+        before = back_order(place - 2)
+
+        @pl.when((place > 1) & deferred(before))
+        def _():
+            send_back(0, before)
+
+        @pl.when(~deferred(slot))
         def _():
             send_back(0, slot)
         return carry
 
     lax.fori_loop(0, 4, grad_step, 0)
     keys(0)
+    hub_back(0)
 
     for r in range(GROUP):
         dq_ref[:, r * DIM:(r + 1) * DIM] = (jnp.transpose(dqt_ref[r]) * SCALE).astype(jnp.bfloat16)
@@ -335,21 +488,22 @@
     dq_near.start()
 
     def late_step(place, carry):
-        slot = order(3 - place)
-
-        @pl.when(has_child(slot))
+        slot = back_order(place + 2)
+
+        @pl.when(deferred(slot))
         def _():
             send_back(0, slot)
         return carry
 
-    lax.fori_loop(0, 4, late_step, 0)
+    lax.fori_loop(0, 2, late_step, 0)
 
     copies = []
     for t, out in ((1, dv_out), (0, dk_out)):
-        for is_there, index in [(given(d), d - 1) for d in range(1, 5)] + [(has_child(0), 4)]:
+        for is_there, index in [(given(d), d - 1) for d in range(1, 5)] + [(edge, 4), ((outer == 3) & (z > 1), 8)]:
             @pl.when(is_there)
             def _(index=index):
-                back_arrived(t, index).wait_recv()
+                for side in range(2):
+                    back_arrived(t, index, side).wait_recv()
                 part_ref[t, 0] += back_ref[t, index].astype(jnp.float32)
         give_ref[t, 0] = part_ref[t, 0].astype(jnp.bfloat16)
         narrow = columns(core * DIM)
@@ -367,6 +521,29 @@
         to_sibling(t).wait_send()
         for copy in heads_to_sibling(t):
             copy.wait_send()
+        @pl.when(chip == 12)
+        def _(t=t):
+            for side in range(2):
+                for copy in hub_sends(t, side):
+                    copy.wait_send()
+
+        for cond, copy in own_hub_sends(t):
+            @pl.when(cond)
+            def _(copy=copy):
+                copy.wait_send()
+
+        @pl.when((chip == 3) & (core == 1))
+        def _(t=t):
+            for slot in range(1, 5):
+                for side in range(2):
+                    round_send(t, slot, side).wait_send()
+
+        @pl.when(chip == 0)
+        def _(t=t):
+            for side in range(2):
+                for copy in hub_back_sends(t, side):
+                    copy.wait_send()
+
         for slot in range(1, 5):
             @pl.when(handed_on(slot))
             def _(slot=slot):
@@ -375,7 +552,8 @@
 
             @pl.when(there(slot))
             def _(slot=slot):
-                give(t, slot).wait_send()
+                for side in range(2):
+                    give(t, slot, side).wait_send()
     for copy in [dq_far, dq_near] + copies:
         copy.wait()
 
@@ -399,10 +577,11 @@
             vmem((10 * GROUP, TOK, ROWS), f32), vmem((10 * GROUP, TOK, ROWS), f32),
             vmem((10 * GROUP, 1, ROWS), f32), vmem((GROUP, 1, ROWS), f32),
             vmem((GROUP, 1, ROWS), f32), vmem((GROUP, 1, ROWS), f32), vmem((1, ROWS), i32),
-            vmem((2, 5, ROWS, DIM), f32), vmem((2, 8, ROWS, DIM), bf16), vmem((2, 5, ROWS, DIM), bf16),
+            vmem((2, 5, ROWS, DIM), f32), vmem((2, 9, ROWS, DIM), bf16), vmem((2, 5, ROWS, DIM), bf16),
             vmem((GROUP, DIM, ROWS), f32), vmem((ROWS, GROUP * DIM), bf16),
-            dma((2 * GROUP + 2,)), dma((2, GROUP)), dma((2, GROUP)), dma((2, 9)), dma((2, 5, 2)), dma((2, 5, 2)),
-            dma((2, 5)), dma((2, 8)), dma((3,)), dma((3,)),
+            dma((2 * GROUP + 2,)), dma((2, GROUP)), dma((2, GROUP)), dma((2, 13)), dma((2, 5, 2)), dma((2, 5, 2)),
+            dma((2, 5, 2)), dma((2, 9, 2)), dma((3,)), dma((3,)),
+            vmem((2, 5, ROWS, DIM), bf16), dma((2, 5, 2)), dma((2, 4, 2)), dma((2, 2, 2)),
         ],
         compiler_params=pltpu.CompilerParams(
             collective_id=0, has_side_effects=True, vmem_limit_bytes=60 << 20),

time: 79.5 us -> 71 us (0.89)
  Pallas kernels: 75.2 us -> 66.7 us
    pallas_call x1, Pallas kernels: 75.2 us -> 66.7 us  [per_device(): pl.pallas_call(kernel, out_shape=(jax.ShapeDtypeStruct(query_states.shape...]
where the time goes in v3:
time: 71 us; the launch traced here: 70.9 us
  Pallas kernels  66.7 us (94%)
  local copies, waits for them, and re-layouts  3.51 us (5%)
    pallas_call x1, Pallas kernels, per_device(): pl.pallas_call(kernel, out_shape=(jax.ShapeDtypeStruct(query_states.shape...  66.7 us
    unnamed x7, local copies, waits for them, and re-layouts  3.51 us

profile of v3, /device:TPU:87, one launch (start us, length us, event | category | flops | bytes accessed | tf_op | source)
XLA Modules:
  0.0 70.9 jit_solution(1836630831297178282)
XLA Ops:
  0.6 66.7 %attention_grads.1 = (bf16[256,1024]{1,0:T(8,128)(2,1)}, bf16[256,256]{1,0:T(8,128)(2,1)}, bf16[256,256]{1,0:T(8,128)(2,1)}) custom-call(s32[65]{0:T(128)} %cu_ref.1, bf16[256,1024]{1,0:T(8,128)(2,1)} %q_in.1, bf16[256,256]{1,0:T(8,128)(2,1)} %k_in.1, bf16[256,256]{1,0:T(8,128)(2,1)} %v_in.1, bf16[256,1024]{1,0:T(8,128)(2,1)} %g_in.1), custom_call_target="tpu_custom_call" | custom-call | tf_op jit(solution)/shard_map/attention_grads/pallas_call | solution.py:565
  67.4 0.0 copy-start.1
  67.4 1.9 %copy.11 = bf16[256,1024]{1,0:T(8,128)(2,1)} copy(bf16[256,1024]{1,0:T(8,128)(2,1)} %get-tuple-element.6) | data formatting | bytes 1048576
  69.3 0.0 copy-done.1
  69.3 0.0 copy-start
  69.3 0.7 copy.12
  70.0 0.3 copy-done
  70.2 0.7 copy.13
Async XLA Ops:
  67.4 1.9 %copy-start.1 = (bf16[256,256]{1,0:T(8,128)(2,1)S(1)}, bf16[256,256]{1,0:T(8,128)(2,1)}, u32[]{:S(2)}) copy-start(bf16[256,256]{1,0:T(8,128)(2,1)} %get-tuple-element.7) | copy-start | bytes 393220
  69.3 1.0 %copy-start = (bf16[256,256]{1,0:T(8,128)(2,1)S(1)}, bf16[256,256]{1,0:T(8,128)(2,1)}, u32[]{:S(2)}) copy-start(bf16[256,256]{1,0:T(8,128)(2,1)} %get-tuple-element.8) | copy-start | bytes 393220

commit v4 on v3

--- a/solution.py
+++ b/solution.py
@@ -27,7 +27,6 @@
 
 
 TAKEN = packed(((4, 3, 2, 1), (2, 4, 1, 3), (2, 1, 4, 3)))
-BACK_FOLD = packed(((3, 4, 1, 2), (4, 3, 2, 1), (4, 2, 1, 3), (2, 3, 4, 1)))
 TAKEN_LAST = packed(((1, 2, 4, 3), (1, 2, 3, 4)))
 
 
@@ -93,12 +92,11 @@
     def handed_on(slot):
         return goes_up(slot) | goes_down(slot)
 
+    joint = jnp.where(fold & (z == 1), 1, 2)
+    has_joint = (z == 1) & (outer != 0) | (z == 2) & (outer != 3)
+
     def has_child(slot):
-        across = (edge & (slot < 4)) | (fold & (z == 2) & (slot > 2))
-        return across | (head & (slot == 3)) | ((slot == 2) & (((z == 2) & (outer != 3)) | ((z == 1) & ~fold & (outer != 0))))
-
-    def deferred(slot):
-        return (edge & (slot < 4)) | (fold & (z == 2) & (slot > 2))
+        return (head & (slot < 4)) | (has_joint & (slot == joint))
 
     def order(place):
         last = jnp.where((z == 3) | chain, 1, 0)
@@ -111,7 +109,7 @@
         return (digits // power) % 4 + 1
 
     def back_order(place):
-        return jnp.where(fold, digit(BACK_FOLD, (z + 2) % 4, place), order(3 - place))
+        return jnp.where(fold & (z == 2), (place + 2) % 4 + 1, order(3 - place))
 
     def half(side):
         return pl.ds(pl.multiple_of(side * TOK, TOK), TOK)
@@ -326,12 +324,13 @@
         return remote(view, view, out_send.at[0], back_recv.at[t, index, side], sibling)
 
     def give(t, slot, side):
-        over = fold & (slot > z)
-        index = jnp.where(z == 0, slot + 3, jnp.where(
-            z == 1, jnp.where(slot == 4, 7, slot + 5), jnp.where(z == 2, 10 - slot, 4)))
+        over = fold & (slot > z) & (z > 0)
+        index = jnp.where(z == 1, slot + 3, jnp.where(z == 2, 10 - slot, 4))
         index = jnp.where(over, index, slot - 1)
-        to = jnp.where(z == 0, 15, jnp.where(z == 1, jnp.where(slot == 4, 16, 18), 0))
-        to = jnp.where(over, to, chip - slot)
+        to = jnp.where(over, jnp.where(z == 1, 16, 0), chip - slot)
+        merged = fold & (z == 2) & (slot == 2)
+        index = jnp.where(merged, 5, index)
+        to = jnp.where(merged, 17, to)
         down = (z == 3) & (slot == 3) & ~edge
         up = (z == 0) & (slot == 1) & ~fold
         index = jnp.where(down | up, 6, index)
@@ -354,12 +353,12 @@
                 give(t, slot, side).start()
 
     def given(d):
-        across = (z + d > 3) & (outer != 3) & (outer != 7)
+        across = ((z + d > 3) & (outer != 3) & (outer != 7)) | ((outer == 3) & (z + d == 4))
         if d == 1:
-            return (z < 3) | (across & (z < 3))
+            return (z < 3) | edge
         if d == 3:
             return ((z == 0) & (outer == 3)) | across
-        return (z + d <= 3) | across
+        return ((z + d <= 3) & ~head) | across
 
     def hub_back_sends(t, side):
         rows = half(side)
@@ -413,7 +412,12 @@
         def _():
             hub(1)
             hub_round(1, (3, 4))
-            take(1, order(0))
+
+        early = jnp.where(chain, place - 1, place - 3)
+
+        @pl.when((early >= 0) & ((early < 2) | edge))
+        def _():
+            take(1, order(early))
 
         units(slot, scores)
         return carry
@@ -434,50 +438,53 @@
         slot = back_order(place)
         values(slot)
 
-        @pl.when(~deferred(slot))
+        @pl.when(~has_child(slot))
         def _():
             send_back(1, slot)
 
+        @pl.when(place == 1)
+        def _():
+            values(0)
+
         units(order(place), prob_grads)
 
-        @pl.when(place < 3)
-        def _():
-            take(1, order(place + 1))
-
-        before = back_order(place - 2)
-
-        @pl.when((place > 1) & deferred(before))
-        def _():
-            send_back(1, before)
+        ahead_of = jnp.where(chain, 2, 1)
+
+        @pl.when((place < 4 - ahead_of) & ~(edge & (place == 0)))
+        def _():
+            take(1, order(place + ahead_of))
         return carry
 
     lax.fori_loop(0, 4, value_step, 0)
-    values(0)
     hub_back(1)
 
     def grad_step(place, carry):
         slot = back_order(place)
         keys(slot)
-        early = back_order(place + 2)
-
-        @pl.when((place < 2) & deferred(early))
-        def _():
-            send_back(1, early)
-
-        before = back_order(place - 2)
-
-        @pl.when((place > 1) & deferred(before))
-        def _():
-            send_back(0, before)
-
-        @pl.when(~deferred(slot))
+
+        @pl.when(~has_child(slot))
         def _():
             send_back(0, slot)
+
+        waiting = jnp.where(head, 3 - place, joint)
+
+        @pl.when((head & (place < 3)) | (has_joint & (place == 3)))
+        def _():
+            send_back(1, waiting)
         return carry
 
     lax.fori_loop(0, 4, grad_step, 0)
     keys(0)
     hub_back(0)
+
+    @pl.when(head)
+    def _():
+        for slot in (3, 2, 1):
+            send_back(0, slot)
+
+    @pl.when(has_joint & ~fold)
+    def _():
+        send_back(0, joint)
 
     for r in range(GROUP):
         dq_ref[:, r * DIM:(r + 1) * DIM] = (jnp.transpose(dqt_ref[r]) * SCALE).astype(jnp.bfloat16)
@@ -487,19 +494,13 @@
     dq_near = pltpu.make_async_copy(dq_ref.at[half(core)], dq_out.at[:, wide], local_sem.at[0])
     dq_near.start()
 
-    def late_step(place, carry):
-        slot = back_order(place + 2)
-
-        @pl.when(deferred(slot))
-        def _():
-            send_back(0, slot)
-        return carry
-
-    lax.fori_loop(0, 2, late_step, 0)
+    @pl.when(has_joint & fold)
+    def _():
+        send_back(0, joint)
 
     copies = []
     for t, out in ((1, dv_out), (0, dk_out)):
-        for is_there, index in [(given(d), d - 1) for d in range(1, 5)] + [(edge, 4), ((outer == 3) & (z > 1), 8)]:
+        for is_there, index in [(given(d), d - 1) for d in range(1, 5)] + [((outer == 3) & (z > 1), 8)]:
             @pl.when(is_there)
             def _(index=index):
                 for side in range(2):

time: 71 us -> 67 us (0.944)
  Pallas kernels: 66.7 us -> 62.6 us
    pallas_call x1, Pallas kernels: 66.7 us -> 62.6 us  [per_device(): pl.pallas_call(kernel, out_shape=(jax.ShapeDtypeStruct(query_states.shape...]
where the time goes in v4:
time: 67 us; the launch traced here: 66.7 us
  Pallas kernels  62.6 us (93%)
  local copies, waits for them, and re-layouts  3.51 us (5%)
    pallas_call x1, Pallas kernels, per_device(): pl.pallas_call(kernel, out_shape=(jax.ShapeDtypeStruct(query_states.shape...  62.6 us
    unnamed x7, local copies, waits for them, and re-layouts  3.51 us

profile of v4, /device:TPU:87, one launch (start us, length us, event | category | flops | bytes accessed | tf_op | source)
XLA Modules:
  0.0 66.7 jit_solution(15336065370729728102)
XLA Ops:
  0.6 62.6 %attention_grads.1 = (bf16[256,1024]{1,0:T(8,128)(2,1)}, bf16[256,256]{1,0:T(8,128)(2,1)}, bf16[256,256]{1,0:T(8,128)(2,1)}) custom-call(s32[65]{0:T(128)} %cu_ref.1, bf16[256,1024]{1,0:T(8,128)(2,1)} %q_in.1, bf16[256,256]{1,0:T(8,128)(2,1)} %k_in.1, bf16[256,256]{1,0:T(8,128)(2,1)} %v_in.1, bf16[256,1024]{1,0:T(8,128)(2,1)} %g_in.1), custom_call_target="tpu_custom_call" | custom-call | tf_op jit(solution)/shard_map/attention_grads/pallas_call | solution.py:566
  63.2 0.0 copy-start.1
  63.2 1.9 %copy.11 = bf16[256,1024]{1,0:T(8,128)(2,1)} copy(bf16[256,1024]{1,0:T(8,128)(2,1)} %get-tuple-element.6) | data formatting | bytes 1048576
  65.1 0.0 copy-done.1
  65.1 0.0 copy-start
  65.1 0.7 copy.12
  65.8 0.3 copy-done
  66.1 0.7 copy.13
Async XLA Ops:
  63.2 1.9 %copy-start.1 = (bf16[256,256]{1,0:T(8,128)(2,1)S(1)}, bf16[256,256]{1,0:T(8,128)(2,1)}, u32[]{:S(2)}) copy-start(bf16[256,256]{1,0:T(8,128)(2,1)} %get-tuple-element.7) | copy-start | bytes 393220
  65.1 1.0 %copy-start = (bf16[256,256]{1,0:T(8,128)(2,1)S(1)}, bf16[256,256]{1,0:T(8,128)(2,1)}, u32[]{:S(2)}) copy-start(bf16[256,256]{1,0:T(8,128)(2,1)} %get-tuple-element.8) | copy-start | bytes 393220

commit v5 on v4

--- a/solution.py
+++ b/solution.py
@@ -318,6 +318,15 @@
                     return acc + dot(ds, qbuf[r])
                 part_ref[0, slot, pl.ds(side * TOK, TOK)] = SCALE * lax.fori_loop(
                     0, GROUP, step, jnp.zeros((TOK, DIM), jnp.float32), unroll=True)
+                send_half(0, slot, side)
+
+    def send_half(t, slot, side):
+        if not isinstance(slot, int):
+            @pl.when(~has_child(slot))
+            def _():
+                rows = half(side)
+                give_ref[t, slot, rows] = part_ref[t, slot, rows].astype(jnp.bfloat16)
+                give(t, slot, side).start()
 
     def back_arrived(t, index, side):
         view = back_ref.at[t, index, half(side)]
@@ -461,11 +470,6 @@
     def grad_step(place, carry):
         slot = back_order(place)
         keys(slot)
-
-        @pl.when(~has_child(slot))
-        def _():
-            send_back(0, slot)
-
         waiting = jnp.where(head, 3 - place, joint)
 
         @pl.when((head & (place < 3)) | (has_joint & (place == 3)))
@@ -559,17 +563,24 @@
         copy.wait()
 
 
+def write_out(dq_in, dk_in, dv_in, dq_out, dk_out, dv_out):
+    dq_out[...] = dq_in[...]
+    dk_out[...] = dk_in[...]
+    dv_out[...] = dv_in[...]
+
+
 def per_device(query_states, key_states, value_states, out_grad, cu_seqlens):
     f32, bf16, i32 = jnp.float32, jnp.bfloat16, jnp.int32
     vmem, dma = pltpu.VMEM, pltpu.SemaphoreType.DMA
     anywhere = pl.BlockSpec(memory_space=pl.ANY)
-    return pl.pallas_call(
+    shapes = (
+        jax.ShapeDtypeStruct(query_states.shape, bf16),
+        jax.ShapeDtypeStruct(key_states.shape, bf16),
+        jax.ShapeDtypeStruct(value_states.shape, bf16),
+    )
+    grads = pl.pallas_call(
         kernel,
-        out_shape=(
-            jax.ShapeDtypeStruct(query_states.shape, bf16),
-            jax.ShapeDtypeStruct(key_states.shape, bf16),
-            jax.ShapeDtypeStruct(value_states.shape, bf16),
-        ),
+        out_shape=shapes,
         in_specs=[pl.BlockSpec(memory_space=pltpu.SMEM)] + [anywhere] * 4,
         out_specs=(anywhere,) * 3,
         scratch_shapes=[
@@ -588,6 +599,11 @@
             collective_id=0, has_side_effects=True, vmem_limit_bytes=60 << 20),
         name="attention_grads",
     )(cu_seqlens, query_states, key_states, value_states, out_grad)
+    rows = query_states.shape[0] // 2
+    specs = tuple(pl.BlockSpec((rows, shape.shape[1]), lambda i: (i, 0)) for shape in shapes)
+    return pl.pallas_call(
+        write_out, grid=(2,), out_shape=shapes, in_specs=list(specs), out_specs=specs, name="write_out",
+    )(*grads)
 
 
 def solution(mesh):

time: 67 us -> 64.9 us (0.969)
  local copies, waits for them, and re-layouts: 3.51 us -> 0 us
  Pallas kernels: 62.6 us -> 64.1 us
    unnamed x7 -> x0, local copies, waits for them, and re-layouts: 3.51 us -> none
    pallas_call x1 -> x2, Pallas kernels: 62.6 us -> 64.1 us  [the longest x1 62.2 us: per_device(): pl.pallas_call(kernel, out_shape=shapes, in_specs=[pl.BlockSpec(memory_sp...]
where the time goes in v5:
time: 64.9 us; the launch traced here: 64.8 us
  Pallas kernels  64.1 us (99%)
    pallas_call x1, Pallas kernels, per_device(): pl.pallas_call(kernel, out_shape=shapes, in_specs=[pl.BlockSpec(memory_sp...  62.2 us
    pallas_call x1, Pallas kernels, per_device(): pl.pallas_call(write_out, grid=(2,), out_shape=shapes, in_specs=list(spec...  1.91 us

profile of v5, /device:TPU:87, one launch (start us, length us, event | category | flops | bytes accessed | tf_op | source)
XLA Modules:
  0.0 64.8 jit_solution(17998107001614504758)
XLA Ops:
  0.6 62.2 %attention_grads.1 = (bf16[256,1024]{1,0:T(8,128)(2,1)}, bf16[256,256]{1,0:T(8,128)(2,1)}, bf16[256,256]{1,0:T(8,128)(2,1)}) custom-call(s32[65]{0:T(128)} %cu_ref.1, bf16[256,1024]{1,0:T(8,128)(2,1)} %q_in.1, bf16[256,256]{1,0:T(8,128)(2,1)} %k_in.1, bf16[256,256]{1,0:T(8,128)(2,1)} %v_in.1, bf16[256,1024]{1,0:T(8,128)(2,1)} %g_in.1), custom_call_target="tpu_custom_call" | custom-call | tf_op jit(solution)/shard_map/attention_grads/pallas_call | solution.py:581
  62.9 1.9 %write_out.1 = (bf16[256,1024]{1,0:T(8,128)(2,1)}, bf16[256,256]{1,0:T(8,128)(2,1)}, bf16[256,256]{1,0:T(8,128)(2,1)}) custom-call(bf16[256,1024]{1,0:T(8,128)(2,1)} %get-tuple-element.6.dq_in, bf16[256,256]{1,0:T(8,128)(2,1)} %get-tuple-element.7.dk_in, bf16[256,256]{1,0:T(8,128)(2,1)} %get-tuple-element.8.dv_in), custom_call_target="tpu_custom_call" | custom-call | tf_op jit(solution)/shard_map/write_out/pallas_call | solution.py:604

commit v6 on v5

--- a/solution.py
+++ b/solution.py
@@ -478,12 +478,17 @@
         return carry
 
     lax.fori_loop(0, 4, grad_step, 0)
+
+    @pl.when(head)
+    def _():
+        send_back(0, 3)
+
     keys(0)
     hub_back(0)
 
     @pl.when(head)
     def _():
-        for slot in (3, 2, 1):
+        for slot in (2, 1):
             send_back(0, slot)
 
     @pl.when(has_joint & ~fold)

time: 64.9 us -> 64.9 us (level)
  no operation moved by 1% of the time
where the time goes in v6:
time: 64.9 us; the launch traced here: 64.8 us
  Pallas kernels  64.1 us (99%)
    pallas_call x1, Pallas kernels, per_device(): pl.pallas_call(kernel, out_shape=shapes, in_specs=[pl.BlockSpec(memory_sp...  62.2 us
    pallas_call x1, Pallas kernels, per_device(): pl.pallas_call(write_out, grid=(2,), out_shape=shapes, in_specs=list(spec...  1.91 us

profile of v6, /device:TPU:87, one launch (start us, length us, event | category | flops | bytes accessed | tf_op | source)
XLA Modules:
  0.0 64.8 jit_solution(15519942279008560068)
XLA Ops:
  0.6 62.2 %attention_grads.1 = (bf16[256,1024]{1,0:T(8,128)(2,1)}, bf16[256,256]{1,0:T(8,128)(2,1)}, bf16[256,256]{1,0:T(8,128)(2,1)}) custom-call(s32[65]{0:T(128)} %cu_ref.1, bf16[256,1024]{1,0:T(8,128)(2,1)} %q_in.1, bf16[256,256]{1,0:T(8,128)(2,1)} %k_in.1, bf16[256,256]{1,0:T(8,128)(2,1)} %v_in.1, bf16[256,1024]{1,0:T(8,128)(2,1)} %g_in.1), custom_call_target="tpu_custom_call" | custom-call | tf_op jit(solution)/shard_map/attention_grads/pallas_call | solution.py:586
  62.9 1.9 %write_out.1 = (bf16[256,1024]{1,0:T(8,128)(2,1)}, bf16[256,256]{1,0:T(8,128)(2,1)}, bf16[256,256]{1,0:T(8,128)(2,1)}) custom-call(bf16[256,1024]{1,0:T(8,128)(2,1)} %get-tuple-element.6.dq_in, bf16[256,256]{1,0:T(8,128)(2,1)} %get-tuple-element.7.dk_in, bf16[256,256]{1,0:T(8,128)(2,1)} %get-tuple-element.8.dv_in), custom_call_target="tpu_custom_call" | custom-call | tf_op jit(solution)/shard_map/write_out/pallas_call | solution.py:609
